TPU v7x, 32 devices: a whole 2x2x4 slice. The times are simulated.
32 devices in a mesh: tm: 8 (over z, core), space: 4 (over y, x).
Axes of the slice: x: 2, y: 2, z: 4, core: 2. Of those that a mesh axis runs over, the one named last changes fastest.
Arguments:
- iterate: float32 [64, 4, 128, 128], P('tm', 'space'), may hold values from -6 to 6
- forcing: float32 [64, 4, 128, 128], P('tm', 'space'), may hold values from -6 to 6
- start_field: float32 [4, 128, 128], P('space'), may hold values from -6 to 6
- classes: int32 [4, 128, 128], P('space'), may hold values from 0 to 7
- open_mask: int32 [4, 128, 128], P('space'), may hold values 0 or 1
- diffusivity: float32 [8], replicated, may hold values from 0.3 to 3
- drift: float32 [3, 8], replicated, may hold values from -0.9 to 0.9
Outputs:
- residual: float32 [64, 4, 128, 128], P('tm', 'space')
- corrected: float32 [64, 4, 128, 128], P('tm', 'space')
All inputs are finite; a program needn't handle non-finite values. No bound on the sum of `open_mask` on one device may be relied on, other than what follows from the above.
Results may differ from a plain program's by a relative error of at most 0.0003.
Values sent between devices are 32-bit elements; how exact they have to be, the bound alone decides.
A program may use at most 64 MiB of HBM per device.

v0:
```python
import math

import jax
import jax.numpy as jnp
from jax import lax
from jax.sharding import PartitionSpec as P

SWEEPS = 4


ALPHA = 0.1


def with_halo(value, sides, width):
    for axis, dim in sides:
        count, length = (lax.axis_size(axis), value.shape[dim])
        up = [(i, (i + 1) % count) for i in range(count - 1)]
        down = [(j, i) for i, j in up]
        last = lax.slice_in_dim(value, length - width, length, axis=dim)
        initial = lax.slice_in_dim(value, 0, width, axis=dim)
        before = lax.ppermute(last, axis, up)
        after = lax.ppermute(initial, axis, down)
        value = jnp.concatenate([before, value, after], axis=dim)
    return value


def shifted(value, axis, by):
    count = lax.axis_size(axis)
    pairs = [(i, i + by) for i in range(count) if 0 <= i + by < count]
    return lax.ppermute(value, axis, pairs)


def step_tables(length):
    index = jnp.arange(length, dtype=jnp.int32)
    folded = index[:, None] * index[None, :] % length
    angle = folded.astype(jnp.float32) * (2.0 * math.pi / length)
    cosine = jnp.cos(angle)
    sine = jnp.sin(angle)
    ramp = jnp.exp(index.astype(jnp.float32) * (math.log(ALPHA) / length))
    forward_re = cosine * ramp[None, :]
    forward_im = -sine * ramp[None, :]
    back_re = cosine / (ramp[:, None] * length)
    back_im = -sine / (ramp[:, None] * length)
    root = math.exp(math.log(ALPHA) / length)
    base = index.astype(jnp.float32) * (2.0 * math.pi / length)
    shift_re = 1.0 - root * jnp.cos(base)
    shift_im = root * jnp.sin(base)
    return (forward_re, forward_im, back_re, back_im, shift_re, shift_im)


def coefficients(classes, open_mask, diffusivity, drift):
    kappa = jnp.zeros(classes.shape, jnp.float32)
    tilt_x = jnp.zeros(classes.shape, jnp.float32)
    tilt_y = jnp.zeros(classes.shape, jnp.float32)
    tilt_z = jnp.zeros(classes.shape, jnp.float32)
    for level in range(diffusivity.shape[0]):
        match = classes == level
        kappa = jnp.where(match, diffusivity[level], kappa)
        tilt_x = jnp.where(match, drift[0, level], tilt_x)
        tilt_y = jnp.where(match, drift[1, level], tilt_y)
        tilt_z = jnp.where(match, drift[2, level], tilt_z)
    weight = open_mask.astype(jnp.float32)
    return (weight, kappa, kappa * tilt_x, kappa * tilt_y, kappa * tilt_z)


def couple(padded, kappa, flow_x, flow_y, flow_z):
    east = padded[..., 2:, 1:-1, 1:-1]
    west = padded[..., :-2, 1:-1, 1:-1]
    north = padded[..., 1:-1, 2:, 1:-1]
    south = padded[..., 1:-1, :-2, 1:-1]
    upper = padded[..., 1:-1, 1:-1, 2:]
    lower = padded[..., 1:-1, 1:-1, :-2]
    total = kappa * (east + west + north + south + upper + lower)
    return total - flow_x * (east - west) - flow_y * (north - south) - flow_z * (upper - lower)


def solve(source, shift_re, shift_im, weight, kappa, flow_x, flow_y, flow_z, extend):
    real_part = shift_re + 6.0 * kappa
    norm = real_part * real_part + shift_im * shift_im
    inv_re = real_part / norm
    inv_im = -shift_im / norm

    def update(total):
        return jnp.stack(
            [
                weight * (total[0] * inv_re - total[1] * inv_im),
                weight * (total[0] * inv_im + total[1] * inv_re),
            ]
        )

    field = update(source)
    for sweep in range(SWEEPS):
        field = update(source + couple(extend(field), kappa, flow_x, flow_y, flow_z))
    return field


def block_extend(field):
    padded = with_halo(field, (("tm", 3), ("space", 2)), 1)
    return jnp.pad(padded, ((0, 0), (0, 0), (0, 0), (0, 0), (1, 1)))


def local(iterate, forcing, start_field, classes, open_mask, diffusivity, drift):
    steps = iterate.shape[0]
    groups = lax.axis_size("tm")
    length = steps * groups
    position = lax.axis_index("tm")
    weight, kappa, flow_x, flow_y, flow_z = coefficients(classes, open_mask, diffusivity, drift)
    arrived = shifted(iterate[-1], "tm", 1)
    first = jnp.where(position == 0, start_field, arrived)
    previous = jnp.concatenate([first[None], iterate[:-1]], axis=0)
    masked = iterate * weight
    padded = with_halo(masked, (("space", 1),), 1)
    padded = jnp.pad(padded, ((0, 0), (0, 0), (1, 1), (1, 1)))
    applied = weight * (6.0 * kappa * masked - couple(padded, kappa, flow_x, flow_y, flow_z))
    residual = weight * (forcing + previous - iterate) - applied
    forward_re, forward_im, back_re, back_im, shift_re, shift_im = step_tables(length)
    cells = lax.all_to_all(residual, "tm", split_axis=2, concat_axis=0, tiled=True)
    flat = cells.reshape(length, -1)
    spec_re = jnp.dot(forward_re, flat, precision=lax.Precision.HIGHEST).reshape(cells.shape)
    spec_im = jnp.dot(forward_im, flat, precision=lax.Precision.HIGHEST).reshape(cells.shape)
    spectrum = jnp.stack([spec_re, spec_im])
    rows = cells.shape[2]
    start = position * rows
    own_kappa = lax.dynamic_slice_in_dim(kappa, start, rows, 1)
    own_weight = lax.dynamic_slice_in_dim(weight, start, rows, 1)
    own_x = lax.dynamic_slice_in_dim(flow_x, start, rows, 1)
    own_y = lax.dynamic_slice_in_dim(flow_y, start, rows, 1)
    own_z = lax.dynamic_slice_in_dim(flow_z, start, rows, 1)
    solved = solve(
        spectrum,
        shift_re.reshape(length, 1, 1, 1),
        shift_im.reshape(length, 1, 1, 1),
        own_weight,
        own_kappa,
        own_x,
        own_y,
        own_z,
        block_extend,
    )
    part_re = solved[0].reshape(length, -1)
    part_im = solved[1].reshape(length, -1)
    combined = jnp.dot(back_re, part_re, precision=lax.Precision.HIGHEST) + jnp.dot(
        back_im, part_im, precision=lax.Precision.HIGHEST
    )
    combined = combined.reshape(solved.shape[1:])
    corrected = lax.all_to_all(combined, "tm", split_axis=0, concat_axis=2, tiled=True)
    return (residual, corrected)


def solution(mesh):
    placed = (
        P("tm", "space", None, None),
        P("tm", "space", None, None),
        P("space", None, None),
        P("space", None, None),
        P("space", None, None),
        P(),
        P(),
    )
    return jax.shard_map(
        local,
        mesh=mesh,
        in_specs=placed,
        out_specs=(P("tm", "space", None, None), P("tm", "space", None, None)),
        check_vma=False,
    )
```

profile of v0, /device:TPU:0, one launch (start us, length us, event | category | flops | bytes accessed | tf_op | source)
XLA Modules:
  0.0 379.7 jit_solution(8934986272389905378)
XLA Ops:
  2.7 4.9 %collective-permute-start.2 = (f32[8,1,128,128]{3,2,1,0:T(8,128)S(1)}, f32[8,1,128,128]{3,2,1,0:T(8,128)S(1)}, u32[]{:S(2)}, u32[]{:S(2)}) collective-permute-start(f32[8,1,128,128]{3,2,1,0:T(8,128)S(1)} %broadcast_multiply_fusion), channel_id=1, source_target_pairs={{0,1},{1,2},{2,3},{4,5},{5,6},{6,7},{8,9},{9,10},{10,11},{12,13},{... | collective-permute-start | bytes 1572872 | tf_op jit(solution)/shard_map/ppermute | solution.py:21
  10.4 2.1 collective-permute-start
  13.9 2.1 fusion.79
  17.7 6.6 %select_select_fusion = (f32[1,128,128]{2,1,0:T(8,128)}, pred[1,128,128]{2,1,0:T(8,128)(4,1)S(1)}, pred[1,128,128]{2,1,0:T(8,128)(4,1)S(1)}, pred[1,128,128]{2,1...) fusion(f32[]{:T(128)} %bitcast.10, f32[]{:T(128)} %bitcast.9, ...), kind=kLoop, calls=%fused_computation.123 | loop fusion | flops 262144 | bytes 262176 | tf_op jit(solution)/shard_map/jit(_where)/select_n | solution.py:58
  24.3 5.1 %multiply_bitcast_fusion = (f32[128,128]{1,0:T(8,128)S(1)}, f32[128,128]{1,0:T(8,128)S(1)}) fusion(pred[1,128,128]{2,1,0:T(8,128)(4,1)S(1)} %get-tuple-element.14, pred[1,128,128]{2,1,0:T(8,128)(4,1)S(1)} %get-tuple-element.13, pred[1,128,128]{2,1,0:T(8,128)(4,1)S(1)} %get-tuple-element.12, pred[1,128,128]{2,1,0:T(8,128)(4,1)S(1)} %get-tuple-element.11, ...), kind=kLoop, calls=%fused_computation.122 | loop fusion | flops 147456 | bytes 262176 | tf_op jit(solution)/shard_map/mul | solution.py:114
  29.4 10.0 %select_multiply_fusion = f32[1,128,128]{2,1,0:T(8,128)S(1)} fusion(pred[1,128,128]{2,1,0:T(8,128)(4,1)S(1)} %get-tuple-element.14, pred[1,128,128]{2,1,0:T(8,128)(4,1)S(1)} %get-tuple-element.13, pred[1,128,128]{2,1,0:T(8,128)(4,1)S(1)} %get-tuple-element.12, pred[1,128,128]{2,1,0:T(8,128)(4,1)S(1)} %get-tuple-element.11, ...), kind=kLoop, calls=%fused_computation.119 | loop fusion | flops 278528 | bytes 196672 | tf_op jit(solution)/shard_map/mul | solution.py:63
  39.4 10.2 %select_multiply_fusion.1 = f32[1,128,128]{2,1,0:T(8,128)S(1)} fusion(pred[1,128,128]{2,1,0:T(8,128)(4,1)S(1)} %get-tuple-element.14, pred[1,128,128]{2,1,0:T(8,128)(4,1)S(1)} %get-tuple-element.13, pred[1,128,128]{2,1,0:T(8,128)(4,1)S(1)} %get-tuple-element.12, pred[1,128,128]{2,1,0:T(8,128)(4,1)S(1)} %get-tuple-element.11, ...), kind=kLoop, calls=%fused_computation.120 | loop fusion | flops 278528 | bytes 196672 | tf_op jit(solution)/shard_map/mul | solution.py:63
  49.6 10.1 %select_multiply_fusion.2 = f32[1,128,128]{2,1,0:T(8,128)S(1)} fusion(pred[1,128,128]{2,1,0:T(8,128)(4,1)S(1)} %get-tuple-element.14, pred[1,128,128]{2,1,0:T(8,128)(4,1)S(1)} %get-tuple-element.13, pred[1,128,128]{2,1,0:T(8,128)(4,1)S(1)} %get-tuple-element.12, pred[1,128,128]{2,1,0:T(8,128)(4,1)S(1)} %get-tuple-element.11, ...), kind=kLoop, calls=%fused_computation.121 | loop fusion | flops 278528 | bytes 196672 | tf_op jit(solution)/shard_map/mul | solution.py:63
  64.0 5.0 %all-to-all-start = ((f32[8,1,128,128]{3,0,1,2:T(8,128)}), f32[8,1,128,128]{3,0,1,2:T(8,128)S(1)}, u32[]{:S(2)}, u32[]{:S(2)}) async-start(f32[8,1,128,128]{3,0,1,2:T(8,128)} %copy.42), calls=%async_computation | async-start | bytes 1048576 | tf_op jit(solution)/shard_map/all_to_all | solution.py:117
  69.9 14.5 %all-to-all-done = f32[8,1,128,128]{3,0,1,2:T(8,128)S(1)} async-done(((f32[8,1,128,128]{3,0,1,2:T(8,128)}), f32[8,1,128,128]{3,0,1,2:T(8,128)S(1)}, u32[]{:S(2)}, u32[]{:S(2)}) %all-to-all-start) | async-done | bytes 524320 | tf_op jit(solution)/shard_map/all_to_all | solution.py:117
  89.6 1.8 collective-permute-done.4
  91.6 4.6 %collective-permute-start.6 = (f32[2,64,1,18,128]{4,1,3,2,0:T(8,128)S(1)}, f32[2,64,1,18,128]{4,1,3,2,0:T(8,128)S(1)}, u32[]{:S(2)}, u32[]{:S(2)}) collective-permute-start(f32[2,64,1,18,128]{4,1,3,2,0:T(8,128)S(1)} %pad_maximum_fusion), channel_id=1, source_target_pairs={{0,1},{1,2},{2,3},{4,5},{5,6},{6,7},{8,9},{9,10},{10,11},{12,13},{... | collective-permute-start | bytes 3538952 | tf_op jit(solution)/shard_map/ppermute | solution.py:21
  97.7 23.2 %collective-permute-done.6 = f32[2,64,1,18,128]{4,1,3,2,0:T(8,128)S(1)} collective-permute-done((f32[2,64,1,18,128]{4,1,3,2,0:T(8,128)S(1)}, f32[2,64,1,18,128]{4,1,3,2,0:T(8,128)S(1)}, u32[]{:S(2)}, u32[]{:S(2)}) %collective-permute-start.6) | collective-permute-done | bytes 1179680 | tf_op jit(solution)/shard_map/ppermute | solution.py:21
  120.9 28.1 %collective-permute-done.5 = f32[2,64,1,18,128]{4,1,3,2,0:T(8,128)S(1)} collective-permute-done((f32[2,64,1,18,128]{4,1,3,2,0:T(8,128)S(1)}, f32[2,64,1,18,128]{4,1,3,2,0:T(8,128)S(1)}, u32[]{:S(2)}, u32[]{:S(2)}) %collective-permute-start.5) | collective-permute-done | bytes 1179680 | tf_op jit(solution)/shard_map/ppermute | solution.py:22
  149.0 4.7 %select_maximum_fusion.15 = f32[2,64,3,18,130]{4,1,3,2,0:T(8,128)S(1)} fusion(f32[2,64,1,18,128]{4,1,3,2,0:T(8,128)S(1)} %collective-permute-done.5, f32[2,64,1,18,128]{4,1,3,2,0:T(8,128)S(1)} %collective-permute-done.6, f32[2,64,1,1,128]{4,1,3,2,0:T(8,128)S(1)} %collective-permute-done.4, f32[2,64,1,1,128]{4,1,3,2,0:T(8,128)S(1)} %collective-permute-done.3, ...), kind=kLoop, calls=%fused_computation.17 | loop fusion | flops 12579840 | bytes 7133184 | tf_op jit(solution)/shard_map/concatenate | solution.py:23
  155.0 3.3 collective-permute-start.7
  159.6 3.8 collective-permute-done.8
  163.5 2.6 collective-permute-start.10
  167.6 22.8 %collective-permute-done.10 = f32[2,64,1,18,128]{4,1,3,2,0:T(8,128)S(1)} collective-permute-done((f32[2,64,1,18,128]{4,1,3,2,0:T(8,128)S(1)}, f32[2,64,1,18,128]{4,1,3,2,0:T(8,128)S(1)}, u32[]{:S(2)}, u32[]{:S(2)}) %collective-permute-start.10) | collective-permute-done | bytes 1179680 | tf_op jit(solution)/shard_map/ppermute | solution.py:21
  190.3 25.5 %collective-permute-done.9 = f32[2,64,1,18,128]{4,1,3,2,0:T(8,128)S(1)} collective-permute-done((f32[2,64,1,18,128]{4,1,3,2,0:T(8,128)S(1)}, f32[2,64,1,18,128]{4,1,3,2,0:T(8,128)S(1)}, u32[]{:S(2)}, u32[]{:S(2)}) %collective-permute-start.9) | collective-permute-done | bytes 1179680 | tf_op jit(solution)/shard_map/ppermute | solution.py:22
  215.8 4.7 %select_maximum_fusion.10 = f32[2,64,3,18,130]{4,1,3,2,0:T(8,128)S(1)} fusion(f32[2,64,1,18,128]{4,1,3,2,0:T(8,128)S(1)} %collective-permute-done.9, f32[2,64,1,18,128]{4,1,3,2,0:T(8,128)S(1)} %collective-permute-done.10, f32[2,64,1,1,128]{4,1,3,2,0:T(8,128)S(1)} %collective-permute-done.8, f32[2,64,1,1,128]{4,1,3,2,0:T(8,128)S(1)} %collective-permute-done.7, ...), kind=kLoop, calls=%fused_computation.12 | loop fusion | flops 12579840 | bytes 7133184 | tf_op jit(solution)/shard_map/concatenate | solution.py:23
  221.8 4.0 %collective-permute-start.11 = (f32[2,64,1,1,128]{4,1,3,2,0:T(8,128)S(1)}, f32[2,64,1,1,128]{4,1,3,2,0:T(8,128)S(1)}, u32[]{:S(2)}, u32[]{:S(2)}) collective-permute-start(f32[2,64,1,1,128]{4,1,3,2,0:T(8,128)S(1)} %get-tuple-element.27), channel_id=1, source_target_pairs={{0,4},{4,8},{8,12},{12,16},{16,20},{20,24},{24,28},{1,5},{5,9},{9,... | collective-permute-start | bytes 196616 | tf_op jit(solution)/shard_map/ppermute | solution.py:21
  227.1 3.8 collective-permute-done.12
  233.8 22.8 %collective-permute-done.14 = f32[2,64,1,18,128]{4,1,3,2,0:T(8,128)S(1)} collective-permute-done((f32[2,64,1,18,128]{4,1,3,2,0:T(8,128)S(1)}, f32[2,64,1,18,128]{4,1,3,2,0:T(8,128)S(1)}, u32[]{:S(2)}, u32[]{:S(2)}) %collective-permute-start.14) | collective-permute-done | bytes 1179680 | tf_op jit(solution)/shard_map/ppermute | solution.py:21
  256.6 25.6 %collective-permute-done.13 = f32[2,64,1,18,128]{4,1,3,2,0:T(8,128)S(1)} collective-permute-done((f32[2,64,1,18,128]{4,1,3,2,0:T(8,128)S(1)}, f32[2,64,1,18,128]{4,1,3,2,0:T(8,128)S(1)}, u32[]{:S(2)}, u32[]{:S(2)}) %collective-permute-start.13) | collective-permute-done | bytes 1179680 | tf_op jit(solution)/shard_map/ppermute | solution.py:22
  282.2 4.7 %select_maximum_fusion.5 = f32[2,64,3,18,130]{4,1,3,2,0:T(8,128)S(1)} fusion(f32[2,64,1,18,128]{4,1,3,2,0:T(8,128)S(1)} %collective-permute-done.13, f32[2,64,1,18,128]{4,1,3,2,0:T(8,128)S(1)} %collective-permute-done.14, f32[2,64,1,1,128]{4,1,3,2,0:T(8,128)S(1)} %collective-permute-done.12, f32[2,64,1,1,128]{4,1,3,2,0:T(8,128)S(1)} %collective-permute-done.11, ...), kind=kLoop, calls=%fused_computation.7 | loop fusion | flops 12579840 | bytes 7133184 | tf_op jit(solution)/shard_map/concatenate | solution.py:23
  288.2 4.0 %collective-permute-start.15 = (f32[2,64,1,1,128]{4,1,3,2,0:T(8,128)S(1)}, f32[2,64,1,1,128]{4,1,3,2,0:T(8,128)S(1)}, u32[]{:S(2)}, u32[]{:S(2)}) collective-permute-start(f32[2,64,1,1,128]{4,1,3,2,0:T(8,128)S(1)} %get-tuple-element.25), channel_id=1, source_target_pairs={{0,4},{4,8},{8,12},{12,16},{16,20},{20,24},{24,28},{1,5},{5,9},{9,... | collective-permute-start | bytes 196616 | tf_op jit(solution)/shard_map/ppermute | solution.py:21
  293.6 4.3 %collective-permute-done.16 = f32[2,64,1,1,128]{4,1,3,2,0:T(8,128)S(1)} collective-permute-done((f32[2,64,1,1,128]{4,1,3,2,0:T(8,128)S(1)}, f32[2,64,1,1,128]{4,1,3,2,0:T(8,128)S(1)}, u32[]{:S(2)}, u32[]{:S(2)}) %collective-permute-start.16) | collective-permute-done | bytes 65568 | tf_op jit(solution)/shard_map/ppermute | solution.py:22
  300.8 22.8 %collective-permute-done.18 = f32[2,64,1,18,128]{4,1,3,2,0:T(8,128)S(1)} collective-permute-done((f32[2,64,1,18,128]{4,1,3,2,0:T(8,128)S(1)}, f32[2,64,1,18,128]{4,1,3,2,0:T(8,128)S(1)}, u32[]{:S(2)}, u32[]{:S(2)}) %collective-permute-start.18) | collective-permute-done | bytes 1179680 | tf_op jit(solution)/shard_map/ppermute | solution.py:21
  323.6 25.6 %collective-permute-done.17 = f32[2,64,1,18,128]{4,1,3,2,0:T(8,128)S(1)} collective-permute-done((f32[2,64,1,18,128]{4,1,3,2,0:T(8,128)S(1)}, f32[2,64,1,18,128]{4,1,3,2,0:T(8,128)S(1)}, u32[]{:S(2)}, u32[]{:S(2)}) %collective-permute-start.17) | collective-permute-done | bytes 1179680 | tf_op jit(solution)/shard_map/ppermute | solution.py:22
  349.2 4.7 %select_maximum_fusion = f32[2,64,3,18,130]{4,1,3,2,0:T(8,128)S(1)} fusion(f32[2,64,1,18,128]{4,1,3,2,0:T(8,128)S(1)} %collective-permute-done.17, f32[2,64,1,18,128]{4,1,3,2,0:T(8,128)S(1)} %collective-permute-done.18, f32[2,64,1,1,128]{4,1,3,2,0:T(8,128)S(1)} %collective-permute-done.16, f32[2,64,1,1,128]{4,1,3,2,0:T(8,128)S(1)} %collective-permute-done.15, ...), kind=kLoop, calls=%fused_computation.2 | loop fusion | flops 12579840 | bytes 7133184 | tf_op jit(solution)/shard_map/concatenate | solution.py:23
  357.7 21.2 %all_to_all.33 = f32[64,1,16,128]{3,2,1,0:T(8,128)S(1)} all-to-all(f32[64,1,16,128]{3,2,1,0:T(8,128)S(1)} %bitcast.127), channel_id=1, replica_groups=mesh['tm'=8,'space'=4] {'tm'}, dimensions={0} | all-to-all | bytes 1048576 | tf_op jit(solution)/shard_map/all_to_all | solution.py:146
  (72 shorter events, 39.4 us)
Async XLA Ops:
  0.6 61.6 %copy-start = (f32[8,1,128,128]{3,2,1,0:T(8,128)S(1)}, f32[8,1,128,128]{3,2,1,0:T(8,128)}, u32[]{:S(2)}) copy-start(f32[8,1,128,128]{3,2,1,0:T(8,128)} %param.7) | copy-start | bytes 1572868
  0.6 61.6 %slice-start = ((f32[8,1,128,128]{3,2,1,0:T(8,128)}), f32[7,1,128,128]{3,2,1,0:T(8,128)S(1)}, s32[]{:S(2)}) async-start(f32[8,1,128,128]{3,2,1,0:T(8,128)} %param.7), calls=%async_computation.2 | async-start | bytes 917504 | tf_op jit(solution)/shard_map/slice | solution.py:110
  0.7 61.6 %copy-start.2 = (f32[8,1,128,128]{3,2,1,0:T(8,128)S(1)}, f32[8,1,128,128]{3,2,1,0:T(8,128)}, u32[]{:S(2)}) copy-start(f32[8,1,128,128]{3,2,1,0:T(8,128)} %param.8) | copy-start | bytes 1572868
  2.7 57.8 %collective-permute-start.2 = (f32[8,1,128,128]{3,2,1,0:T(8,128)S(1)}, f32[8,1,128,128]{3,2,1,0:T(8,128)S(1)}, u32[]{:S(2)}, u32[]{:S(2)}) collective-permute-start(f32[8,1,128,128]{3,2,1,0:T(8,128)S(1)} %broadcast_multiply_fusion), channel_id=1, source_target_pairs={{0,1},{1,2},{2,3},{4,5},{5,6},{6,7},{8,9},{9,10},{10,11},{12,13},{... | collective-permute-start | bytes 1572872 | tf_op jit(solution)/shard_map/ppermute | solution.py:21
  7.6 53.0 %collective-permute-start.1 = (f32[8,1,128,128]{3,2,1,0:T(8,128)S(1)}, f32[8,1,128,128]{3,2,1,0:T(8,128)S(1)}, u32[]{:S(2)}, u32[]{:S(2)}) collective-permute-start(f32[8,1,128,128]{3,2,1,0:T(8,128)S(1)} %broadcast_multiply_fusion), channel_id=1, source_target_pairs={{1,0},{2,1},{3,2},{5,4},{6,5},{7,6},{9,8},{10,9},{11,10},{13,12},{... | collective-permute-start | bytes 1572872 | tf_op jit(solution)/shard_map/ppermute | solution.py:22
  10.4 49.3 %collective-permute-start = (f32[1,128,128]{2,1,0:T(8,128)}, f32[1,128,128]{2,1,0:T(8,128)}, u32[]{:S(2)}, u32[]{:S(2)}) collective-permute-start(f32[1,128,128]{2,1,0:T(8,128)} %slice_bitcast_fusion), channel_id=1, source_target_pairs={{0,4},{4,8},{8,12},{12,16},{16,20},{20,24},{24,28},{1,5},{5,9},{9,... | collective-permute-start | bytes 196616 | tf_op jit(solution)/shard_map/ppermute | solution.py:30
  62.9 34.8 %copy-start.1 = (f32[8,1,128,128]{3,2,1,0:T(8,128)}, f32[8,1,128,128]{3,2,1,0:T(8,128)S(1)}, u32[]{:S(2)}) copy-start(f32[8,1,128,128]{3,2,1,0:T(8,128)S(1)} %fusion.20) | copy-start | bytes 1572868
  64.0 20.4 %all-to-all-start = ((f32[8,1,128,128]{3,0,1,2:T(8,128)}), f32[8,1,128,128]{3,0,1,2:T(8,128)S(1)}, u32[]{:S(2)}, u32[]{:S(2)}) async-start(f32[8,1,128,128]{3,0,1,2:T(8,128)} %copy.42), calls=%async_computation | async-start | bytes 1048576 | tf_op jit(solution)/shard_map/all_to_all | solution.py:117
  86.8 2.9 collective-permute-start.3
  88.3 3.1 collective-permute-start.4
  91.6 29.4 %collective-permute-start.6 = (f32[2,64,1,18,128]{4,1,3,2,0:T(8,128)S(1)}, f32[2,64,1,18,128]{4,1,3,2,0:T(8,128)S(1)}, u32[]{:S(2)}, u32[]{:S(2)}) collective-permute-start(f32[2,64,1,18,128]{4,1,3,2,0:T(8,128)S(1)} %pad_maximum_fusion), channel_id=1, source_target_pairs={{0,1},{1,2},{2,3},{4,5},{5,6},{6,7},{8,9},{9,10},{10,11},{12,13},{... | collective-permute-start | bytes 3538952 | tf_op jit(solution)/shard_map/ppermute | solution.py:21
  96.2 52.8 %collective-permute-start.5 = (f32[2,64,1,18,128]{4,1,3,2,0:T(8,128)S(1)}, f32[2,64,1,18,128]{4,1,3,2,0:T(8,128)S(1)}, u32[]{:S(2)}, u32[]{:S(2)}) collective-permute-start(f32[2,64,1,18,128]{4,1,3,2,0:T(8,128)S(1)} %pad_maximum_fusion), channel_id=1, source_target_pairs={{1,0},{2,1},{3,2},{5,4},{6,5},{7,6},{9,8},{10,9},{11,10},{13,12},{... | collective-permute-start | bytes 3538952 | tf_op jit(solution)/shard_map/ppermute | solution.py:22
  155.0 4.6 %collective-permute-start.7 = (f32[2,64,1,1,128]{4,1,3,2,0:T(8,128)S(1)}, f32[2,64,1,1,128]{4,1,3,2,0:T(8,128)S(1)}, u32[]{:S(2)}, u32[]{:S(2)}) collective-permute-start(f32[2,64,1,1,128]{4,1,3,2,0:T(8,128)S(1)} %get-tuple-element.29), channel_id=1, source_target_pairs={{0,4},{4,8},{8,12},{12,16},{16,20},{20,24},{24,28},{1,5},{5,9},{9,... | collective-permute-start | bytes 196616 | tf_op jit(solution)/shard_map/ppermute | solution.py:21
  158.3 5.1 %collective-permute-start.8 = (f32[2,64,1,1,128]{4,1,3,2,0:T(8,128)S(1)}, f32[2,64,1,1,128]{4,1,3,2,0:T(8,128)S(1)}, u32[]{:S(2)}, u32[]{:S(2)}) collective-permute-start(f32[2,64,1,1,128]{4,1,3,2,0:T(8,128)S(1)} %get-tuple-element.30), channel_id=1, source_target_pairs={{4,0},{8,4},{12,8},{16,12},{20,16},{24,20},{28,24},{5,1},{9,5},{13... | collective-permute-start | bytes 196616 | tf_op jit(solution)/shard_map/ppermute | solution.py:22
  163.5 26.8 %collective-permute-start.10 = (f32[2,64,1,18,128]{4,1,3,2,0:T(8,128)S(1)}, f32[2,64,1,18,128]{4,1,3,2,0:T(8,128)S(1)}, u32[]{:S(2)}, u32[]{:S(2)}) collective-permute-start(f32[2,64,1,18,128]{4,1,3,2,0:T(8,128)S(1)} %pad_maximum_fusion.1), channel_id=1, source_target_pairs={{0,1},{1,2},{2,3},{4,5},{5,6},{6,7},{8,9},{9,10},{10,11},{12,13},{... | collective-permute-start | bytes 3538952 | tf_op jit(solution)/shard_map/ppermute | solution.py:21
  166.1 49.7 %collective-permute-start.9 = (f32[2,64,1,18,128]{4,1,3,2,0:T(8,128)S(1)}, f32[2,64,1,18,128]{4,1,3,2,0:T(8,128)S(1)}, u32[]{:S(2)}, u32[]{:S(2)}) collective-permute-start(f32[2,64,1,18,128]{4,1,3,2,0:T(8,128)S(1)} %pad_maximum_fusion.1), channel_id=1, source_target_pairs={{1,0},{2,1},{3,2},{5,4},{6,5},{7,6},{9,8},{10,9},{11,10},{13,12},{... | collective-permute-start | bytes 3538952 | tf_op jit(solution)/shard_map/ppermute | solution.py:22
  221.8 5.4 %collective-permute-start.11 = (f32[2,64,1,1,128]{4,1,3,2,0:T(8,128)S(1)}, f32[2,64,1,1,128]{4,1,3,2,0:T(8,128)S(1)}, u32[]{:S(2)}, u32[]{:S(2)}) collective-permute-start(f32[2,64,1,1,128]{4,1,3,2,0:T(8,128)S(1)} %get-tuple-element.27), channel_id=1, source_target_pairs={{0,4},{4,8},{8,12},{12,16},{16,20},{20,24},{24,28},{1,5},{5,9},{9,... | collective-permute-start | bytes 196616 | tf_op jit(solution)/shard_map/ppermute | solution.py:21
  225.8 5.1 %collective-permute-start.12 = (f32[2,64,1,1,128]{4,1,3,2,0:T(8,128)S(1)}, f32[2,64,1,1,128]{4,1,3,2,0:T(8,128)S(1)}, u32[]{:S(2)}, u32[]{:S(2)}) collective-permute-start(f32[2,64,1,1,128]{4,1,3,2,0:T(8,128)S(1)} %get-tuple-element.28), channel_id=1, source_target_pairs={{4,0},{8,4},{12,8},{16,12},{20,16},{24,20},{28,24},{5,1},{9,5},{13... | collective-permute-start | bytes 196616 | tf_op jit(solution)/shard_map/ppermute | solution.py:22
  231.0 25.6 %collective-permute-start.14 = (f32[2,64,1,18,128]{4,1,3,2,0:T(8,128)S(1)}, f32[2,64,1,18,128]{4,1,3,2,0:T(8,128)S(1)}, u32[]{:S(2)}, u32[]{:S(2)}) collective-permute-start(f32[2,64,1,18,128]{4,1,3,2,0:T(8,128)S(1)} %pad_maximum_fusion.2), channel_id=1, source_target_pairs={{0,1},{1,2},{2,3},{4,5},{5,6},{6,7},{8,9},{9,10},{10,11},{12,13},{... | collective-permute-start | bytes 3538952 | tf_op jit(solution)/shard_map/ppermute | solution.py:21
  232.5 49.7 %collective-permute-start.13 = (f32[2,64,1,18,128]{4,1,3,2,0:T(8,128)S(1)}, f32[2,64,1,18,128]{4,1,3,2,0:T(8,128)S(1)}, u32[]{:S(2)}, u32[]{:S(2)}) collective-permute-start(f32[2,64,1,18,128]{4,1,3,2,0:T(8,128)S(1)} %pad_maximum_fusion.2), channel_id=1, source_target_pairs={{1,0},{2,1},{3,2},{5,4},{6,5},{7,6},{9,8},{10,9},{11,10},{13,12},{... | collective-permute-start | bytes 3538952 | tf_op jit(solution)/shard_map/ppermute | solution.py:22
  288.2 5.4 %collective-permute-start.15 = (f32[2,64,1,1,128]{4,1,3,2,0:T(8,128)S(1)}, f32[2,64,1,1,128]{4,1,3,2,0:T(8,128)S(1)}, u32[]{:S(2)}, u32[]{:S(2)}) collective-permute-start(f32[2,64,1,1,128]{4,1,3,2,0:T(8,128)S(1)} %get-tuple-element.25), channel_id=1, source_target_pairs={{0,4},{4,8},{8,12},{12,16},{16,20},{20,24},{24,28},{1,5},{5,9},{9,... | collective-permute-start | bytes 196616 | tf_op jit(solution)/shard_map/ppermute | solution.py:21
  292.2 5.6 %collective-permute-start.16 = (f32[2,64,1,1,128]{4,1,3,2,0:T(8,128)S(1)}, f32[2,64,1,1,128]{4,1,3,2,0:T(8,128)S(1)}, u32[]{:S(2)}, u32[]{:S(2)}) collective-permute-start(f32[2,64,1,1,128]{4,1,3,2,0:T(8,128)S(1)} %get-tuple-element.26), channel_id=1, source_target_pairs={{4,0},{8,4},{12,8},{16,12},{20,16},{24,20},{28,24},{5,1},{9,5},{13... | collective-permute-start | bytes 196616 | tf_op jit(solution)/shard_map/ppermute | solution.py:22
  298.0 25.6 %collective-permute-start.18 = (f32[2,64,1,18,128]{4,1,3,2,0:T(8,128)S(1)}, f32[2,64,1,18,128]{4,1,3,2,0:T(8,128)S(1)}, u32[]{:S(2)}, u32[]{:S(2)}) collective-permute-start(f32[2,64,1,18,128]{4,1,3,2,0:T(8,128)S(1)} %pad_maximum_fusion.3), channel_id=1, source_target_pairs={{0,1},{1,2},{2,3},{4,5},{5,6},{6,7},{8,9},{9,10},{10,11},{12,13},{... | collective-permute-start | bytes 3538952 | tf_op jit(solution)/shard_map/ppermute | solution.py:21
  299.5 49.7 %collective-permute-start.17 = (f32[2,64,1,18,128]{4,1,3,2,0:T(8,128)S(1)}, f32[2,64,1,18,128]{4,1,3,2,0:T(8,128)S(1)}, u32[]{:S(2)}, u32[]{:S(2)}) collective-permute-start(f32[2,64,1,18,128]{4,1,3,2,0:T(8,128)S(1)} %pad_maximum_fusion.3), channel_id=1, source_target_pairs={{1,0},{2,1},{3,2},{5,4},{6,5},{7,6},{9,8},{10,9},{11,10},{13,12},{... | collective-permute-start | bytes 3538952 | tf_op jit(solution)/shard_map/ppermute | solution.py:22
where the time goes:
time: 381 us; the launch traced here: 380 us
  waiting for transfers between devices  225 us (59%)
  other arithmetic  72.2 us (19%)
  starting transfers between devices  46.9 us (12%)
  blocking collectives  21.2 us (6%)
  local copies, waits for them, and re-layouts  9.92 us (3%)
    ppermute x9, waiting for transfers between devices, with_halo(): after = lax.ppermute(initial, axis, down)  118 us
    ppermute x9, waiting for transfers between devices, with_halo(): before = lax.ppermute(last, axis, up)  91.6 us
    mul x3, other arithmetic, coefficients(): return (weight, kappa, kappa * tilt_x, kappa * tilt_y, kappa * tilt_z)  30.3 us
    ppermute x9, starting transfers between devices, with_halo(): before = lax.ppermute(last, axis, up)  28 us
    all_to_all x1, blocking collectives, local(): lax.all_to_all(combined, 'tm', split_axis=0, concat_axis=2, tiled=True)  21.2 us
    concatenate x9, other arithmetic, with_halo(): value = jnp.concatenate([before, value, after], axis=dim)  20.8 us
    all_to_all x1, waiting for transfers between devices, local(): lax.all_to_all(residual, 'tm', split_axis=2, concat_axis=0, tiled=True)  14.5 us
    ppermute x9, starting transfers between devices, with_halo(): after = lax.ppermute(initial, axis, down)  11.8 us
  transfers between devices with their start and end apart: 20, of which 13 were waited for; matrix products, arithmetic and copies ran while one was open for 13% of the time, Pallas kernels for 0%

commit v1 on v0

v1 whole, which is shorter than its diff:
```python
import functools
import math

import jax
import jax.numpy as jnp
import numpy as np
from jax import lax
from jax.experimental import pallas as pl
from jax.experimental.pallas import tpu as pltpu
from jax.sharding import PartitionSpec as P

SWEEPS = 4
ALPHA = 0.1
PAD = 8
MESH = pl.DeviceIdType.MESH


def step_tables(length, shares):
    half = length // 2
    planes = length // shares
    own = planes // 2
    index = np.arange(length)
    ramp = ALPHA ** (index / length)
    freq = np.arange(half)
    angle = 2.0 * math.pi * ((freq[:, None] * index[None, :]) % length) / length
    other = np.cos(math.pi * index)
    f_re, f_im = np.cos(angle), -np.sin(angle)
    f_im[0] = other
    scale = np.where(freq == 0, 1.0, 2.0)[:, None]
    b_re, b_im = scale * f_re, scale * f_im
    order = lambda re, im: np.stack([re.reshape(shares, own, -1), im.reshape(shares, own, -1)], 1).reshape(length, -1)
    forward = order(f_re, f_im) * ramp[None, :]
    back = (order(b_re, b_im) / (ramp[None, :] * length)).T
    root = ALPHA ** (1.0 / length)
    base = 2.0 * math.pi * freq / length
    re = 1.0 - root * np.cos(base)
    second = re.copy()
    second[0] = 1.0 + root
    im = root * np.sin(base)
    shifts = np.stack([re, second, im])[:, :, None].astype(np.float32)
    return forward.astype(np.float32), back.astype(np.float32), shifts


def kernel(T, S, it_ref, fc_ref, start_ref, cm_ref, diff_ref, drift_ref, fwd_ref, back_ref, shift_ref,
           res_ref, cor_ref,
           masked, last, arrived, cA, cB, xe, xw, xin, xout, xc, own_c, tin, spec, src, f0, f1,
           sol_c, inv, spec2, outb, ssem, rsem):
    NY, N, NZ = it_ref.shape
    L = N * T
    RB, Q = NY // T, T // S
    XB = Q * RB
    G = L // S
    H = G // 2
    W = SWEEPS
    R = RB + 2 * W
    t, s = lax.axis_index("tm"), lax.axis_index("space")

    barrier = pltpu.get_barrier_semaphore()
    for k in range(1, S):
        pl.semaphore_signal(barrier, inc=1, device_id={"space": lax.rem(s + k, S)}, device_id_type=MESH)
    for k in range(1, T):
        pl.semaphore_signal(barrier, inc=1, device_id={"tm": lax.rem(t + k, T)}, device_id_type=MESH)

    used = [0]
    sent = []

    def remote(a, b, where):
        at = used[0]
        used[0] += 1
        copy = pltpu.make_async_remote_copy(src_ref=a, dst_ref=b, send_sem=ssem.at[at], recv_sem=rsem.at[at],
                                            device_id=where, device_id_type=MESH)
        copy.start()
        sent.append(copy)
        return copy

    def table(cls, ref_row):
        out = jnp.zeros(cls.shape, jnp.float32)
        for level in range(diff_ref.shape[0]):
            out = jnp.where(cls == level, ref_row(level), out)
        return out

    def mult(v, m):
        return pl.multiple_of(v, m)

    lane = lax.broadcasted_iota(jnp.int32, (1, NZ), 1)
    not_top = jnp.where(lane < NZ - 1, 1.0, 0.0)
    not_low = jnp.where(lane > 0, 1.0, 0.0)

    cls = cm_ref[0, PAD:PAD + NY, :]
    own_c[0] = cm_ref[1, PAD:PAD + NY, :].astype(jnp.float32)
    kappa = table(cls, lambda i: diff_ref[i])
    fy = kappa * table(cls, lambda i: drift_ref[1, i])
    fz = kappa * table(cls, lambda i: drift_ref[2, i])
    own_c[1] = 6.0 * kappa
    own_c[2] = kappa - fy
    own_c[3] = kappa + fy
    own_c[4] = (kappa - fz) * not_top
    own_c[5] = (kappa + fz) * not_low
    zero = jnp.zeros((N, NZ), jnp.float32)
    masked[0] = zero
    masked[NY + 1] = zero

    def mask_row(r, c):
        masked[r + 1] = it_ref[r] * own_c[0, pl.ds(r, 1), :]
        return c

    lax.fori_loop(0, NY, mask_row, 0, unroll=8)
    last[...] = it_ref[:, N - 1, :]

    pl.semaphore_wait(barrier, S - 1 + T - 1)

    cpA = [remote(cm_ref.at[:, pl.ds(mult(lax.rem(s + k, S) * XB + PAD, 8), XB)], cA.at[s],
                  {"space": lax.rem(s + k, S)}) for k in range(1, S)]
    there = []
    for jj in range(Q):
        j = lax.rem(t + jj, Q)
        there.append([remote(masked.at[pl.ds((Q * lax.rem(s + k, S) + j) * RB + 1, RB)],
                             xin.at[s, pl.ds(jj * RB, RB)], {"space": lax.rem(s + k, S)}) for k in range(1, S)])
    cpL = remote(last, arrived, {"tm": lax.rem(t + 1, T)})
    cpB = [remote(cm_ref.at[:, pl.ds(mult(RB * t, 8), RB + 2 * PAD)], cB.at[s], {"space": lax.rem(s + k, S)})
           for k in range(1, S)]

    cA[s] = cm_ref[:, pl.ds(mult(s * XB + PAD, 8), XB), :]
    cB[s] = cm_ref[:, pl.ds(mult(RB * t, 8), RB + 2 * PAD), :]
    for jj in range(Q):
        j = lax.rem(t + jj, Q)
        xin[s, pl.ds(jj * RB, RB)] = masked[pl.ds((Q * s + j) * RB + 1, RB)]
    for cp in cpA:
        cp.wait_recv()

    def x_coefficients(x, c):
        cls = cA[x, 0]
        kappa = table(cls, lambda i: diff_ref[i])
        fx = kappa * table(cls, lambda i: drift_ref[0, i])
        xe[x] = kappa - fx
        xw[x] = kappa + fx
        return c

    lax.fori_loop(0, S, x_coefficients, 0)

    backs = []
    for jj in range(Q):
        j = lax.rem(t + jj, Q)
        for cp in there[jj]:
            cp.wait_recv()

        def x_row(r, c):
            at = jj * RB + r
            row = j * RB + r
            for x in range(S):
                total = None
                if x + 1 < S:
                    total = xe[x, pl.ds(row, 1), :] * xin[x + 1, at]
                if x > 0:
                    term = xw[x, pl.ds(row, 1), :] * xin[x - 1, at]
                    total = term if total is None else total + term
                xout[x, at] = zero if total is None else total
            return c

        lax.fori_loop(0, RB, x_row, 0, unroll=4)
        backs.append([remote(xout.at[lax.rem(s + k, S), pl.ds(jj * RB, RB)], xc.at[pl.ds((Q * s + j) * RB, RB)],
                             {"space": lax.rem(s + k, S)}) for k in range(1, S)])
        xc[pl.ds((Q * s + j) * RB, RB)] = xout[s, pl.ds(jj * RB, RB)]

    cpL.wait_recv()
    cpL.wait_send()
    sent[:] = [copy for copy in sent if copy is not cpL]
    last[...] = jnp.where(t == 0, start_ref[...], arrived[...])
    first = lax.broadcasted_iota(jnp.int32, (N, NZ), 0) == 0

    def residual_row(r):
        it = it_ref[r]
        mk = masked[r + 1]
        co = lambda i: own_c[i, pl.ds(r, 1), :]
        previous = jnp.where(first, last[pl.ds(r, 1), :], pltpu.roll(it, 1, 0))
        cpl = co(2) * masked[r + 2] + co(3) * masked[r] + xc[r]
        cpl = cpl + co(4) * pltpu.roll(mk, NZ - 1, 1) + co(5) * pltpu.roll(mk, 1, 1)
        return co(0) * ((fc_ref[r] + previous - it) - (co(1) * mk - cpl))

    tms = []
    for jj in range(Q):
        for cp in backs[jj]:
            cp.wait_recv()
        for m in list(range(1, S)) + [0]:
            k = jj + Q * m
            to = lax.rem(t + k, T)

            def one(r, c):
                res_ref[to * RB + r] = residual_row(to * RB + r)
                return c

            lax.fori_loop(0, RB, one, 0, unroll=4)
            if k:
                tms.append(remote(res_ref.at[pl.ds(to * RB, RB)], tin.at[:, pl.ds(mult(N * t, 8), N), :], {"tm": to}))
            else:
                tin[:, pl.ds(mult(N * t, 8), N), :] = res_ref[pl.ds(to * RB, RB)]

    for cp in cpB:
        cp.wait_recv()

    def solve_coefficients(x, c):
        cls = cB[x, 0]
        kappa = table(cls, lambda i: diff_ref[i])
        fx = kappa * table(cls, lambda i: drift_ref[0, i])
        fy = kappa * table(cls, lambda i: drift_ref[1, i])
        fz = kappa * table(cls, lambda i: drift_ref[2, i])
        sol_c[0, x] = kappa - fx
        sol_c[1, x] = kappa + fx
        sol_c[2, x] = kappa - fy
        sol_c[3, x] = kappa + fy
        sol_c[4, x] = (kappa - fz) * not_top
        sol_c[5, x] = (kappa + fz) * not_low
        sol_c[6, x] = cB[x, 1].astype(jnp.float32)
        sol_c[7, x] = 6.0 * kappa
        return c

    lax.fori_loop(0, S, solve_coefficients, 0)
    own = pl.ds(mult(s * H, 8) if H % 8 == 0 else s * H, H)
    sh_re, sh_second, sh_im = shift_ref[0, own], shift_ref[1, own], shift_ref[2, own]

    def inverse_row(r, c):
        for x in range(S):
            k6 = sol_c[7, x, pl.ds(r + PAD - W, 1), :]
            w = sol_c[6, x, pl.ds(r + PAD - W, 1), :]
            a, b = sh_re + k6, sh_second + k6
            na = w / (a * a + sh_im * sh_im)
            nb = w / (b * b + sh_im * sh_im)
            inv[0, x, r] = a * na
            inv[1, x, r] = -sh_im * na
            inv[2, x, r] = b * nb
        return c

    lax.fori_loop(0, R, inverse_row, 0)

    for cp in tms:
        cp.wait_recv()

    def transform(matrix_ref, a, b):
        group = 4 if RB % 4 == 0 else 1
        for g in range(0, RB, group):
            wide = jnp.concatenate([a[g + i] for i in range(group)], axis=1)
            wide = jnp.dot(matrix_ref[...], wide, precision=lax.Precision.HIGHEST, preferred_element_type=jnp.float32)
            for i in range(group):
                b[g + i] = wide[:, i * NZ:(i + 1) * NZ]

    transform(fwd_ref, tin, spec)
    def planes(who):
        return pl.ds(mult(G * who, 8), G)

    cps = [remote(spec.at[:, planes(lax.rem(s + k, S)), :], src.at[s, pl.ds(W, RB)], {"space": lax.rem(s + k, S)})
           for k in range(1, S)]
    src[s, pl.ds(W, RB)] = spec[:, planes(s), :]
    for cp in cps:
        cp.wait_recv()
    halos = [remote(src.at[:, pl.ds(W, W)], src.at[:, pl.ds(RB + W, W)], {"tm": lax.rem(t + T - 1, T)}),
             remote(src.at[:, pl.ds(RB, W)], src.at[:, pl.ds(0, W)], {"tm": lax.rem(t + 1, T)})]

    def update(x, r, total, out):
        re, im = total[:H], total[H:]
        a, b, d = inv[0, x, r], inv[1, x, r], inv[2, x, r]
        out[x, r] = jnp.concatenate([re * a - im * b, re * b + im * d], axis=0)

    def first_row(r, c):
        for x in range(S):
            update(x, r, src[x, r], f0)
        return c

    lax.fori_loop(W, W + RB, first_row, 0, unroll=2)
    for cp in halos:
        cp.wait_recv()
    lax.fori_loop(0, W, first_row, 0, unroll=2)
    lax.fori_loop(W + RB, R, first_row, 0, unroll=2)

    old, new = f0, f1
    for sweep in range(1, SWEEPS + 1):
        def sweep_row(r, c):
            for x in range(S):
                co = lambda i: sol_c[i, x, pl.ds(r + PAD - W, 1), :]
                mid = old[x, r]
                total = src[x, r] + co(2) * old[x, r + 1] + co(3) * old[x, r - 1]
                total = total + co(4) * pltpu.roll(mid, NZ - 1, 1) + co(5) * pltpu.roll(mid, 1, 1)
                if x + 1 < S:
                    total = total + co(0) * old[x + 1, r]
                if x > 0:
                    total = total + co(1) * old[x - 1, r]
                update(x, r, total, new)
            return c

        lax.fori_loop(sweep, R - sweep, sweep_row, 0, unroll=2)
        old, new = new, old

    cps = [remote(old.at[lax.rem(s + k, S), pl.ds(W, RB)], spec2.at[:, planes(s), :], {"space": lax.rem(s + k, S)})
           for k in range(1, S)]
    spec2[:, planes(s), :] = old[s, pl.ds(W, RB)]
    for cp in cps:
        cp.wait_recv()
    transform(back_ref, spec2, outb)
    cps = []
    for k in range(1, T):
        to = lax.rem(t + k, T)
        cps.append(remote(outb.at[:, pl.ds(mult(N * to, 8), N), :], cor_ref.at[pl.ds(RB * t, RB)], {"tm": to}))
    cor_ref[pl.ds(RB * t, RB)] = outb[:, pl.ds(mult(N * t, 8), N), :]
    for cp in cps:
        cp.wait_recv()
    for cp in sent:
        cp.wait_send()


def local(T, S, iterate, forcing, start_field, classes, open_mask, diffusivity, drift):
    N, _, NY, NZ = iterate.shape
    L = N * T
    RB, Q = NY // T, T // S
    XB, G = Q * RB, L // S
    H, W = G // 2, SWEEPS
    R = RB + 2 * W
    fwd, back, shifts = step_tables(L, S)
    shifts = np.ascontiguousarray(np.broadcast_to(shifts, (3, L // 2, NZ)))
    it = jnp.swapaxes(iterate[:, 0], 0, 1)
    fc = jnp.swapaxes(forcing[:, 0], 0, 1)
    cm = jnp.pad(jnp.concatenate([classes, open_mask], 0), ((0, 0), (PAD, PAD), (0, 0)))
    copies = 3 * (S - 1) + 1 + 2 * Q * (S - 1) + (S - 1) + 2 + 2 * (T - 1)
    f32 = jnp.float32
    vmem = lambda *shape: pltpu.VMEM(shape, f32)
    VM, SM = pl.BlockSpec(memory_space=pltpu.VMEM), pl.BlockSpec(memory_space=pltpu.SMEM)
    res, cor = pl.pallas_call(
        functools.partial(kernel, T, S),
        out_shape=[jax.ShapeDtypeStruct((NY, N, NZ), f32)] * 2,
        in_specs=[VM, VM, VM, VM, SM, SM, VM, VM, VM],
        out_specs=[VM, VM],
        scratch_shapes=[
            vmem(NY + 2, N, NZ), vmem(NY, NZ), vmem(NY, NZ),
            pltpu.VMEM((S, 2, XB, NZ), jnp.int32), pltpu.VMEM((S, 2, RB + 2 * PAD, NZ), jnp.int32),
            vmem(S, XB, NZ), vmem(S, XB, NZ), vmem(S, XB, N, NZ), vmem(S, XB, N, NZ), vmem(NY, N, NZ),
            vmem(6, NY, NZ), vmem(RB, L, NZ), vmem(RB, L, NZ),
            vmem(S, R, G, NZ), vmem(S, R, G, NZ), vmem(S, R, G, NZ),
            vmem(8, S, RB + 2 * PAD, NZ), vmem(3, S, R, H, NZ), vmem(RB, L, NZ), vmem(RB, L, NZ),
            pltpu.SemaphoreType.DMA((copies,)), pltpu.SemaphoreType.DMA((copies,)),
        ],
        compiler_params=pltpu.CompilerParams(collective_id=0, has_side_effects=True, vmem_limit_bytes=48 * 2**20),
        name="all_at_once",
    )(it, fc, start_field[0], cm, diffusivity, drift, fwd, back, shifts)
    return jnp.swapaxes(res, 0, 1)[:, None], jnp.swapaxes(cor, 0, 1)[:, None]


def solution(mesh):
    field, cells = P("tm", "space", None, None), P("space", None, None)
    return jax.shard_map(
        functools.partial(local, mesh.shape["tm"], mesh.shape["space"]),
        mesh=mesh,
        in_specs=(field, field, cells, cells, cells, P(), P()),
        out_specs=(field, field),
        check_vma=False,
    )
```

time: 381 us -> 75.1 us (0.20)
  the two profiles are of different devices: /device:TPU:0 before, /device:TPU:9 now
where the time goes in v1:
time: 75.1 us; the launch traced here: 75 us
  Pallas kernels  69.1 us (92%)
  local copies, waits for them, and re-layouts  4.25 us (6%)
  other arithmetic  0.94 us (1%)
    pallas_call x1, Pallas kernels, local(): pl.pallas_call(functools.partial(kernel, T, S), out_shape=[jax.ShapeDtype...  69.1 us
    unnamed x16, local copies, waits for them, and re-layouts  2.56 us
    transpose x1, local copies, waits for them, and re-layouts, local(): fc = jnp.swapaxes(forcing[:, 0], 0, 1)  1.69 us

profile of v1, /device:TPU:9, one launch (start us, length us, event | category | flops | bytes accessed | tf_op | source)
XLA Modules:
  0.0 75.0 jit_solution(14166995884843391710)
XLA Ops:
  0.6 0.0 copy-start.6
  0.6 0.9 %pad_add_fusion = s32[2,128,128]{2,1,0:T(8,128)S(1)} fusion(s32[1,128,128]{2,1,0:T(8,128)} %param.14, s32[1,128,128]{2,1,0:T(8,128)} %param.13), kind=kLoop, calls=%fused_computation.2 | loop fusion | flops 32768 | bytes 262144 | tf_op jit(solution)/shard_map/concatenate | solution.py:320
  1.6 0.1 copy-done.6
  1.7 0.0 copy-start
  1.7 0.0 copy-start.1
  1.7 0.0 copy-start.2
  1.7 0.0 copy-start.3
  1.7 1.7 %copy_bitcast_fusion = (f32[128,8,128]{2,1,0:T(8,128)S(1)}, f32[128,8,128]{2,1,0:T(8,128)S(1)}) fusion(f32[8,1,128,128]{3,2,1,0:T(8,128)S(1)} %copy-done.6, f32[8,1,128,128]{3,2,1,0:T(8,128)} %param.10), kind=kLoop, calls=%fused_computation | loop fusion | bytes 2097152 | tf_op jit(solution)/shard_map/transpose | solution.py:319
  3.4 0.0 copy-start.4
  3.4 0.0 copy-start.5
  3.5 0.0 copy-done
  3.5 0.0 copy-done.1
  3.5 0.0 copy-done.2
  3.5 0.0 copy-done.3
  3.5 0.6 copy-done.4
  4.1 0.0 copy-done.5
  4.1 69.1 %all_at_once.1 = (f32[128,8,128]{2,1,0:T(8,128)S(1)}, f32[128,8,128]{2,1,0:T(8,128)S(1)}) custom-call(f32[128,8,128]{2,1,0:T(8,128)S(1)} %get-tuple-element.9.it_ref, f32[128,8,128]{2,1,0:T(8,128)S(1)} %get-tuple-element.8.fc_ref, f32[128,128]{1,0:T(8,128)S(1)} %bitcast.17, s32[2,144,128]{2,1,0:T(8,128)S(1)} %pad.4.cm_ref, f32[8]{0:T(128)S(1)} %copy-done.5, ...), custom_call_target="tpu_custom_call" | custom-call | tf_op jit(solution)/shard_map/all_at_once/pallas_call | solution.py:325
  73.2 0.9 %copy.14 = f32[8,1,128,128]{3,2,1,0:T(8,128)} copy(f32[8,1,128,128]{3,0,2,1:T(8,128)S(1)} %bitcast.16) | data formatting | bytes 1048576
  74.1 0.9 %copy.15 = f32[8,1,128,128]{3,2,1,0:T(8,128)} copy(f32[8,1,128,128]{3,0,2,1:T(8,128)S(1)} %bitcast.15) | data formatting | bytes 1048576
  (1 shorter events, 0.0 us)
Async XLA Ops:
  0.6 1.1 %copy-start.6 = (f32[8,1,128,128]{3,2,1,0:T(8,128)S(1)}, f32[8,1,128,128]{3,2,1,0:T(8,128)}, u32[]{:S(2)}) copy-start(f32[8,1,128,128]{3,2,1,0:T(8,128)} %param.11) | copy-start | bytes 1572868
  1.7 1.7 %copy-start = (f32[1,128,128]{2,1,0:T(8,128)S(1)}, f32[1,128,128]{2,1,0:T(8,128)}, u32[]{:S(2)}) copy-start(f32[1,128,128]{2,1,0:T(8,128)} %param.12) | copy-start | bytes 196612
  1.7 1.7 %copy-start.1 = (f32[3,32,128]{2,1,0:T(8,128)S(1)}, f32[3,32,128]{2,1,0:T(8,128)}, u32[]{:S(2)}) copy-start(f32[3,32,128]{2,1,0:T(8,128)} %constant.10.clone.shift_ref) | copy-start | bytes 147460
  1.7 1.7 %copy-start.2 = (f32[64,64]{1,0:T(8,128)S(1)}, f32[64,64]{1,0:T(8,128)}, u32[]{:S(2)}) copy-start(f32[64,64]{1,0:T(8,128)} %constant.9.clone.back_ref) | copy-start | bytes 49156
  1.7 1.7 %copy-start.3 = (f32[64,64]{1,0:T(8,128)S(1)}, f32[64,64]{1,0:T(8,128)}, u32[]{:S(2)}) copy-start(f32[64,64]{1,0:T(8,128)} %constant.8.clone.fwd_ref) | copy-start | bytes 49156
  3.4 0.7 copy-start.4
  3.4 0.7 copy-start.5

commit v2 on v1

--- a/solution.py
+++ b/solution.py
@@ -41,9 +41,9 @@
     return forward.astype(np.float32), back.astype(np.float32), shifts
 
 
-def kernel(T, S, it_ref, fc_ref, start_ref, cm_ref, diff_ref, drift_ref, fwd_ref, back_ref, shift_ref,
+def kernel(T, S, it_ref, fc_ref, start_ref, cls_ref, open_ref, diff_ref, drift_ref, fwd_ref, back_ref, shift_ref,
            res_ref, cor_ref,
-           masked, last, arrived, cA, cB, xe, xw, xin, xout, xc, own_c, tin, spec, src, f0, f1,
+           cm_ref, masked, last, arrived, cA, cB, xe, xw, xin, xout, xc, own_c, tin, spec, src, f0, f1,
            sol_c, inv, spec2, outb, ssem, rsem):
     NY, N, NZ = it_ref.shape
     L = N * T
@@ -53,6 +53,8 @@
     H = G // 2
     W = SWEEPS
     R = RB + 2 * W
+    C = RB // W
+    chunks = [0, C - 1] + list(range(1, C - 1))
     t, s = lax.axis_index("tm"), lax.axis_index("space")
 
     barrier = pltpu.get_barrier_semaphore()
@@ -86,8 +88,13 @@
     not_top = jnp.where(lane < NZ - 1, 1.0, 0.0)
     not_low = jnp.where(lane > 0, 1.0, 0.0)
 
-    cls = cm_ref[0, PAD:PAD + NY, :]
-    own_c[0] = cm_ref[1, PAD:PAD + NY, :].astype(jnp.float32)
+    edge = jnp.zeros((PAD, NZ), jnp.int32)
+    for i, ref in enumerate((cls_ref, open_ref)):
+        cm_ref[i, 0:PAD, :] = edge
+        cm_ref[i, PAD + NY:, :] = edge
+        cm_ref[i, PAD:PAD + NY, :] = ref[...]
+    cls = cls_ref[...]
+    own_c[0] = open_ref[...].astype(jnp.float32)
     kappa = table(cls, lambda i: diff_ref[i])
     fy = kappa * table(cls, lambda i: drift_ref[1, i])
     fz = kappa * table(cls, lambda i: drift_ref[2, i])
@@ -111,11 +118,12 @@
 
     cpA = [remote(cm_ref.at[:, pl.ds(mult(lax.rem(s + k, S) * XB + PAD, 8), XB)], cA.at[s],
                   {"space": lax.rem(s + k, S)}) for k in range(1, S)]
+    pieces = [(c, jj) for c in chunks for jj in range(Q)]
     there = []
-    for jj in range(Q):
+    for c, jj in pieces:
         j = lax.rem(t + jj, Q)
-        there.append([remote(masked.at[pl.ds((Q * lax.rem(s + k, S) + j) * RB + 1, RB)],
-                             xin.at[s, pl.ds(jj * RB, RB)], {"space": lax.rem(s + k, S)}) for k in range(1, S)])
+        there.append([remote(masked.at[pl.ds((Q * lax.rem(s + k, S) + j) * RB + c * W + 1, W)],
+                             xin.at[s, pl.ds(jj * RB + c * W, W)], {"space": lax.rem(s + k, S)}) for k in range(1, S)])
     cpL = remote(last, arrived, {"tm": lax.rem(t + 1, T)})
     cpB = [remote(cm_ref.at[:, pl.ds(mult(RB * t, 8), RB + 2 * PAD)], cB.at[s], {"space": lax.rem(s + k, S)})
            for k in range(1, S)]
@@ -139,28 +147,26 @@
     lax.fori_loop(0, S, x_coefficients, 0)
 
     backs = []
-    for jj in range(Q):
+    for (c, jj), copies in zip(pieces, there):
         j = lax.rem(t + jj, Q)
-        for cp in there[jj]:
-            cp.wait_recv()
-
-        def x_row(r, c):
-            at = jj * RB + r
-            row = j * RB + r
+        for cp in copies:
+            cp.wait_recv()
+        base = jj * RB + c * W
+        for r in range(W):
+            row = j * RB + c * W + r
+            fields = [xin[x, base + r] for x in range(S)]
             for x in range(S):
                 total = None
                 if x + 1 < S:
-                    total = xe[x, pl.ds(row, 1), :] * xin[x + 1, at]
+                    total = xe[x, pl.ds(row, 1), :] * fields[x + 1]
                 if x > 0:
-                    term = xw[x, pl.ds(row, 1), :] * xin[x - 1, at]
+                    term = xw[x, pl.ds(row, 1), :] * fields[x - 1]
                     total = term if total is None else total + term
-                xout[x, at] = zero if total is None else total
-            return c
-
-        lax.fori_loop(0, RB, x_row, 0, unroll=4)
-        backs.append([remote(xout.at[lax.rem(s + k, S), pl.ds(jj * RB, RB)], xc.at[pl.ds((Q * s + j) * RB, RB)],
-                             {"space": lax.rem(s + k, S)}) for k in range(1, S)])
-        xc[pl.ds((Q * s + j) * RB, RB)] = xout[s, pl.ds(jj * RB, RB)]
+                xout[x, base + r] = zero if total is None else total
+        home = pl.ds((Q * s + j) * RB + c * W, W)
+        backs.append([remote(xout.at[lax.rem(s + k, S), pl.ds(base, W)], xc.at[home], {"space": lax.rem(s + k, S)})
+                      for k in range(1, S)])
+        xc[home] = xout[s, pl.ds(base, W)]
 
     cpL.wait_recv()
     cpL.wait_send()
@@ -177,23 +183,21 @@
         cpl = cpl + co(4) * pltpu.roll(mk, NZ - 1, 1) + co(5) * pltpu.roll(mk, 1, 1)
         return co(0) * ((fc_ref[r] + previous - it) - (co(1) * mk - cpl))
 
-    tms = []
-    for jj in range(Q):
-        for cp in backs[jj]:
+    tms = {c: [] for c in chunks}
+    for (c, jj), copies in zip(pieces, backs):
+        for cp in copies:
             cp.wait_recv()
         for m in list(range(1, S)) + [0]:
             k = jj + Q * m
             to = lax.rem(t + k, T)
-
-            def one(r, c):
-                res_ref[to * RB + r] = residual_row(to * RB + r)
-                return c
-
-            lax.fori_loop(0, RB, one, 0, unroll=4)
+            at = to * RB + c * W
+            for r in range(W):
+                res_ref[at + r] = residual_row(at + r)
+            here = tin.at[pl.ds(c * W, W), pl.ds(mult(N * t, 8), N), :]
             if k:
-                tms.append(remote(res_ref.at[pl.ds(to * RB, RB)], tin.at[:, pl.ds(mult(N * t, 8), N), :], {"tm": to}))
+                tms[c].append(remote(res_ref.at[pl.ds(at, W)], here, {"tm": to}))
             else:
-                tin[:, pl.ds(mult(N * t, 8), N), :] = res_ref[pl.ds(to * RB, RB)]
+                here[...] = res_ref[pl.ds(at, W)]
 
     for cp in cpB:
         cp.wait_recv()
@@ -232,28 +236,14 @@
 
     lax.fori_loop(0, R, inverse_row, 0)
 
-    for cp in tms:
-        cp.wait_recv()
-
-    def transform(matrix_ref, a, b):
-        group = 4 if RB % 4 == 0 else 1
-        for g in range(0, RB, group):
-            wide = jnp.concatenate([a[g + i] for i in range(group)], axis=1)
-            wide = jnp.dot(matrix_ref[...], wide, precision=lax.Precision.HIGHEST, preferred_element_type=jnp.float32)
-            for i in range(group):
-                b[g + i] = wide[:, i * NZ:(i + 1) * NZ]
-
-    transform(fwd_ref, tin, spec)
+    def transform(matrix_ref, a, b, c):
+        wide = jnp.concatenate([a[c * W + i] for i in range(W)], axis=1)
+        wide = jnp.dot(matrix_ref[...], wide, precision=lax.Precision.HIGHEST, preferred_element_type=jnp.float32)
+        for i in range(W):
+            b[c * W + i] = wide[:, i * NZ:(i + 1) * NZ]
+
     def planes(who):
         return pl.ds(mult(G * who, 8), G)
-
-    cps = [remote(spec.at[:, planes(lax.rem(s + k, S)), :], src.at[s, pl.ds(W, RB)], {"space": lax.rem(s + k, S)})
-           for k in range(1, S)]
-    src[s, pl.ds(W, RB)] = spec[:, planes(s), :]
-    for cp in cps:
-        cp.wait_recv()
-    halos = [remote(src.at[:, pl.ds(W, W)], src.at[:, pl.ds(RB + W, W)], {"tm": lax.rem(t + T - 1, T)}),
-             remote(src.at[:, pl.ds(RB, W)], src.at[:, pl.ds(0, W)], {"tm": lax.rem(t + 1, T)})]
 
     def update(x, r, total, out):
         re, im = total[:H], total[H:]
@@ -265,42 +255,73 @@
             update(x, r, src[x, r], f0)
         return c
 
-    lax.fori_loop(W, W + RB, first_row, 0, unroll=2)
+    halos = []
+
+    def land(c, copies):
+        for cp in copies:
+            cp.wait_recv()
+        if c == 0:
+            halos.append(remote(src.at[:, pl.ds(W, W)], src.at[:, pl.ds(RB + W, W)], {"tm": lax.rem(t + T - 1, T)}))
+        if c == C - 1:
+            halos.append(remote(src.at[:, pl.ds(RB, W)], src.at[:, pl.ds(0, W)], {"tm": lax.rem(t + 1, T)}))
+        lax.fori_loop(W + c * W, W + c * W + W, first_row, 0, unroll=2)
+
+    flying = []
+    for c in chunks:
+        for cp in tms[c]:
+            cp.wait_recv()
+        transform(fwd_ref, tin, spec, c)
+        rows, there_rows = pl.ds(c * W, W), pl.ds(W + c * W, W)
+        copies = [remote(spec.at[rows, planes(lax.rem(s + k, S)), :], src.at[s, there_rows],
+                         {"space": lax.rem(s + k, S)}) for k in range(1, S)]
+        src[s, there_rows] = spec[rows, planes(s), :]
+        if flying:
+            land(*flying.pop())
+        flying.append((c, copies))
+    land(*flying.pop())
     for cp in halos:
         cp.wait_recv()
     lax.fori_loop(0, W, first_row, 0, unroll=2)
     lax.fori_loop(W + RB, R, first_row, 0, unroll=2)
 
     old, new = f0, f1
+    solved = []
     for sweep in range(1, SWEEPS + 1):
         def sweep_row(r, c):
+            mids = [old[x, r] for x in range(S)]
             for x in range(S):
                 co = lambda i: sol_c[i, x, pl.ds(r + PAD - W, 1), :]
-                mid = old[x, r]
                 total = src[x, r] + co(2) * old[x, r + 1] + co(3) * old[x, r - 1]
-                total = total + co(4) * pltpu.roll(mid, NZ - 1, 1) + co(5) * pltpu.roll(mid, 1, 1)
+                total = total + co(4) * pltpu.roll(mids[x], NZ - 1, 1) + co(5) * pltpu.roll(mids[x], 1, 1)
                 if x + 1 < S:
-                    total = total + co(0) * old[x + 1, r]
+                    total = total + co(0) * mids[x + 1]
                 if x > 0:
-                    total = total + co(1) * old[x - 1, r]
+                    total = total + co(1) * mids[x - 1]
                 update(x, r, total, new)
             return c
 
-        lax.fori_loop(sweep, R - sweep, sweep_row, 0, unroll=2)
+        if sweep < SWEEPS:
+            lax.fori_loop(sweep, R - sweep, sweep_row, 0, unroll=2)
+        else:
+            for c in range(C):
+                lax.fori_loop(W + c * W, W + c * W + W, sweep_row, 0, unroll=2)
+                rows, from_rows = pl.ds(c * W, W), pl.ds(W + c * W, W)
+                solved.append([remote(new.at[lax.rem(s + k, S), from_rows], spec2.at[rows, planes(s), :],
+                                      {"space": lax.rem(s + k, S)}) for k in range(1, S)])
+                spec2[rows, planes(s), :] = new[s, from_rows]
         old, new = new, old
 
-    cps = [remote(old.at[lax.rem(s + k, S), pl.ds(W, RB)], spec2.at[:, planes(s), :], {"space": lax.rem(s + k, S)})
-           for k in range(1, S)]
-    spec2[:, planes(s), :] = old[s, pl.ds(W, RB)]
-    for cp in cps:
-        cp.wait_recv()
-    transform(back_ref, spec2, outb)
-    cps = []
-    for k in range(1, T):
-        to = lax.rem(t + k, T)
-        cps.append(remote(outb.at[:, pl.ds(mult(N * to, 8), N), :], cor_ref.at[pl.ds(RB * t, RB)], {"tm": to}))
-    cor_ref[pl.ds(RB * t, RB)] = outb[:, pl.ds(mult(N * t, 8), N), :]
-    for cp in cps:
+    final = []
+    for c in range(C):
+        for cp in solved[c]:
+            cp.wait_recv()
+        transform(back_ref, spec2, outb, c)
+        rows, home = pl.ds(c * W, W), pl.ds(RB * t + c * W, W)
+        for k in range(1, T):
+            to = lax.rem(t + k, T)
+            final.append(remote(outb.at[rows, pl.ds(mult(N * to, 8), N), :], cor_ref.at[home], {"tm": to}))
+        cor_ref[home] = outb[rows, pl.ds(mult(N * t, 8), N), :]
+    for cp in final:
         cp.wait_recv()
     for cp in sent:
         cp.wait_send()
@@ -317,18 +338,18 @@
     shifts = np.ascontiguousarray(np.broadcast_to(shifts, (3, L // 2, NZ)))
     it = jnp.swapaxes(iterate[:, 0], 0, 1)
     fc = jnp.swapaxes(forcing[:, 0], 0, 1)
-    cm = jnp.pad(jnp.concatenate([classes, open_mask], 0), ((0, 0), (PAD, PAD), (0, 0)))
-    copies = 3 * (S - 1) + 1 + 2 * Q * (S - 1) + (S - 1) + 2 + 2 * (T - 1)
+    C = RB // W
+    copies = 2 * (S - 1) + 1 + 2 * C * Q * (S - 1) + 2 * C * (S - 1) + 2 + 2 * C * (T - 1)
     f32 = jnp.float32
     vmem = lambda *shape: pltpu.VMEM(shape, f32)
     VM, SM = pl.BlockSpec(memory_space=pltpu.VMEM), pl.BlockSpec(memory_space=pltpu.SMEM)
     res, cor = pl.pallas_call(
         functools.partial(kernel, T, S),
         out_shape=[jax.ShapeDtypeStruct((NY, N, NZ), f32)] * 2,
-        in_specs=[VM, VM, VM, VM, SM, SM, VM, VM, VM],
+        in_specs=[VM, VM, VM, VM, VM, SM, SM, VM, VM, VM],
         out_specs=[VM, VM],
         scratch_shapes=[
-            vmem(NY + 2, N, NZ), vmem(NY, NZ), vmem(NY, NZ),
+            pltpu.VMEM((2, NY + 2 * PAD, NZ), jnp.int32), vmem(NY + 2, N, NZ), vmem(NY, NZ), vmem(NY, NZ),
             pltpu.VMEM((S, 2, XB, NZ), jnp.int32), pltpu.VMEM((S, 2, RB + 2 * PAD, NZ), jnp.int32),
             vmem(S, XB, NZ), vmem(S, XB, NZ), vmem(S, XB, N, NZ), vmem(S, XB, N, NZ), vmem(NY, N, NZ),
             vmem(6, NY, NZ), vmem(RB, L, NZ), vmem(RB, L, NZ),
@@ -338,7 +359,7 @@
         ],
         compiler_params=pltpu.CompilerParams(collective_id=0, has_side_effects=True, vmem_limit_bytes=48 * 2**20),
         name="all_at_once",
-    )(it, fc, start_field[0], cm, diffusivity, drift, fwd, back, shifts)
+    )(it, fc, start_field[0], classes[0], open_mask[0], diffusivity, drift, fwd, back, shifts)
     return jnp.swapaxes(res, 0, 1)[:, None], jnp.swapaxes(cor, 0, 1)[:, None]
 
 

time: 75.1 us -> 63.3 us (0.84)
  the two profiles are of different devices: /device:TPU:9 before, /device:TPU:0 now
where the time goes in v2:
time: 63.3 us; the launch traced here: 63.1 us
  Pallas kernels  58.1 us (92%)
  local copies, waits for them, and re-layouts  4.31 us (7%)
  between operations  0.75 us (1%)
    pallas_call x1, Pallas kernels, local(): pl.pallas_call(functools.partial(kernel, T, S), out_shape=[jax.ShapeDtype...  58.1 us
    unnamed x18, local copies, waits for them, and re-layouts  2.42 us
    transpose x1, local copies, waits for them, and re-layouts, local(): fc = jnp.swapaxes(forcing[:, 0], 0, 1)  1.89 us

profile of v2, /device:TPU:0, one launch (start us, length us, event | category | flops | bytes accessed | tf_op | source)
XLA Modules:
  0.0 63.1 jit_solution(5194719429320909667)
XLA Ops:
  0.6 0.0 copy-start
  0.6 0.0 copy-start.1
  0.7 0.0 copy-start.2
  0.7 0.0 copy-start.3
  0.7 0.0 copy-start.4
  0.7 0.0 copy-start.5
  0.7 1.9 %copy_bitcast_fusion = (f32[128,8,128]{2,1,0:T(8,128)S(1)}, f32[128,8,128]{2,1,0:T(8,128)S(1)}) fusion(f32[8,1,128,128]{3,2,1,0:T(8,128)} %param.11, f32[8,1,128,128]{3,2,1,0:T(8,128)} %param.10), kind=kLoop, calls=%fused_computation | loop fusion | bytes 2097152 | tf_op jit(solution)/shard_map/transpose | solution.py:340
  2.6 0.0 copy-start.6
  2.6 0.0 copy-start.7
  2.6 0.0 copy-done
  2.6 0.0 copy-done.1
  2.6 0.0 copy-done.2
  2.6 0.0 copy-done.3
  2.7 0.0 copy-done.4
  2.7 0.0 copy-done.5
  2.7 0.6 copy-done.6
  3.3 0.0 copy-done.7
  3.3 58.1 %all_at_once.1 = (f32[128,8,128]{2,1,0:T(8,128)S(1)}, f32[128,8,128]{2,1,0:T(8,128)S(1)}) custom-call(f32[128,8,128]{2,1,0:T(8,128)S(1)} %get-tuple-element.9.it_ref, f32[128,8,128]{2,1,0:T(8,128)S(1)} %get-tuple-element.8.fc_ref, f32[128,128]{1,0:T(8,128)S(1)} %bitcast.19, s32[128,128]{1,0:T(8,128)S(1)} %bitcast.20, s32[128,128]{1,0:T(8,128)S(1)} %bitcast.21, ...), custom_call_target="tpu_custom_call" | custom-call | tf_op jit(solution)/shard_map/all_at_once/pallas_call | solution.py:346
  61.3 0.9 %copy.14 = f32[8,1,128,128]{3,2,1,0:T(8,128)} copy(f32[8,1,128,128]{3,0,2,1:T(8,128)S(1)} %bitcast.18) | data formatting | bytes 1048576
  62.2 0.9 %copy.15 = f32[8,1,128,128]{3,2,1,0:T(8,128)} copy(f32[8,1,128,128]{3,0,2,1:T(8,128)S(1)} %bitcast.17) | data formatting | bytes 1048576
Async XLA Ops:
  0.6 2.0 %copy-start = (f32[1,128,128]{2,1,0:T(8,128)S(1)}, f32[1,128,128]{2,1,0:T(8,128)}, u32[]{:S(2)}) copy-start(f32[1,128,128]{2,1,0:T(8,128)} %param.12) | copy-start | bytes 196612
  0.6 2.0 %copy-start.1 = (s32[1,128,128]{2,1,0:T(8,128)S(1)}, s32[1,128,128]{2,1,0:T(8,128)}, u32[]{:S(2)}) copy-start(s32[1,128,128]{2,1,0:T(8,128)} %param.13) | copy-start | bytes 196612
  0.7 2.0 %copy-start.2 = (s32[1,128,128]{2,1,0:T(8,128)S(1)}, s32[1,128,128]{2,1,0:T(8,128)}, u32[]{:S(2)}) copy-start(s32[1,128,128]{2,1,0:T(8,128)} %param.14) | copy-start | bytes 196612
  0.7 2.0 %copy-start.3 = (f32[3,32,128]{2,1,0:T(8,128)S(1)}, f32[3,32,128]{2,1,0:T(8,128)}, u32[]{:S(2)}) copy-start(f32[3,32,128]{2,1,0:T(8,128)} %constant.8.clone.shift_ref) | copy-start | bytes 147460
  0.7 2.0 %copy-start.4 = (f32[64,64]{1,0:T(8,128)S(1)}, f32[64,64]{1,0:T(8,128)}, u32[]{:S(2)}) copy-start(f32[64,64]{1,0:T(8,128)} %constant.7.clone.back_ref) | copy-start | bytes 49156
  0.7 2.0 %copy-start.5 = (f32[64,64]{1,0:T(8,128)S(1)}, f32[64,64]{1,0:T(8,128)}, u32[]{:S(2)}) copy-start(f32[64,64]{1,0:T(8,128)} %constant.6.clone.fwd_ref) | copy-start | bytes 49156
  2.6 0.7 %copy-start.6 = (f32[3,8]{1,0:T(4,128)S(1)}, f32[3,8]{1,0:T(4,128)}, u32[]{:S(2)}) copy-start(f32[3,8]{1,0:T(4,128)} %drift_ref.1) | copy-start | bytes 292
  2.6 0.7 %copy-start.7 = (f32[8]{0:T(128)S(1)}, f32[8]{0:T(128)}, u32[]{:S(2)}) copy-start(f32[8]{0:T(128)} %diff_ref.1) | copy-start | bytes 100

commit v3 on v2

--- a/solution.py
+++ b/solution.py
@@ -3,6 +3,7 @@
 
 import jax
 import jax.numpy as jnp
+import ml_dtypes
 import numpy as np
 from jax import lax
 from jax.experimental import pallas as pl
@@ -38,12 +39,18 @@
     second[0] = 1.0 + root
     im = root * np.sin(base)
     shifts = np.stack([re, second, im])[:, :, None].astype(np.float32)
-    return forward.astype(np.float32), back.astype(np.float32), shifts
-
-
-def kernel(T, S, it_ref, fc_ref, start_ref, cls_ref, open_ref, diff_ref, drift_ref, fwd_ref, back_ref, shift_ref,
+    return split_matrix(forward), split_matrix(back), shifts
+
+
+def split_matrix(matrix):
+    high = matrix.astype(ml_dtypes.bfloat16)
+    low = (matrix - high.astype(np.float64)).astype(ml_dtypes.bfloat16)
+    return np.concatenate([high, high, low], axis=1)
+
+
+def kernel(T, S, it_in, fc_in, start_ref, cls_ref, open_ref, diff_ref, drift_ref, fwd_ref, back_ref, shift_ref,
            res_ref, cor_ref,
-           cm_ref, masked, last, arrived, cA, cB, xe, xw, xin, xout, xc, own_c, tin, spec, src, f0, f1,
+           it_ref, fc_ref, in_sem, cm_ref, masked, last, arrived, cA, cB, xe, xw, xin, xout, xc, own_c, tin, spec, src, f0, f1,
            sol_c, inv, spec2, outb, ssem, rsem):
     NY, N, NZ = it_ref.shape
     L = N * T
@@ -56,6 +63,12 @@
     C = RB // W
     chunks = [0, C - 1] + list(range(1, C - 1))
     t, s = lax.axis_index("tm"), lax.axis_index("space")
+
+    loads = []
+    for i, (a, b) in enumerate(((it_in, it_ref), (fc_in, fc_ref))):
+        loads.append([pltpu.make_async_copy(a.at[n], b.at[:, n, :], in_sem.at[i * N + n]) for n in range(N)])
+        for copy in loads[i]:
+            copy.start()
 
     barrier = pltpu.get_barrier_semaphore()
     for k in range(1, S):
@@ -107,12 +120,14 @@
     masked[0] = zero
     masked[NY + 1] = zero
 
+    for copy in loads[0]:
+        copy.wait()
+
     def mask_row(r, c):
         masked[r + 1] = it_ref[r] * own_c[0, pl.ds(r, 1), :]
         return c
 
     lax.fori_loop(0, NY, mask_row, 0, unroll=8)
-    last[...] = it_ref[:, N - 1, :]
 
     pl.semaphore_wait(barrier, S - 1 + T - 1)
 
@@ -120,19 +135,22 @@
                   {"space": lax.rem(s + k, S)}) for k in range(1, S)]
     pieces = [(c, jj) for c in chunks for jj in range(Q)]
     there = []
-    for c, jj in pieces:
+
+    def send_piece(c, jj):
         j = lax.rem(t + jj, Q)
         there.append([remote(masked.at[pl.ds((Q * lax.rem(s + k, S) + j) * RB + c * W + 1, W)],
                              xin.at[s, pl.ds(jj * RB + c * W, W)], {"space": lax.rem(s + k, S)}) for k in range(1, S)])
-    cpL = remote(last, arrived, {"tm": lax.rem(t + 1, T)})
+        xin[s, pl.ds(jj * RB + c * W, W)] = masked[pl.ds((Q * s + j) * RB + c * W + 1, W)]
+
+    ahead, lag = 4, 2
+    for piece in pieces[:ahead]:
+        send_piece(*piece)
+    cpL = remote(it_in.at[N - 1], arrived, {"tm": lax.rem(t + 1, T)})
     cpB = [remote(cm_ref.at[:, pl.ds(mult(RB * t, 8), RB + 2 * PAD)], cB.at[s], {"space": lax.rem(s + k, S)})
            for k in range(1, S)]
 
     cA[s] = cm_ref[:, pl.ds(mult(s * XB + PAD, 8), XB), :]
     cB[s] = cm_ref[:, pl.ds(mult(RB * t, 8), RB + 2 * PAD), :]
-    for jj in range(Q):
-        j = lax.rem(t + jj, Q)
-        xin[s, pl.ds(jj * RB, RB)] = masked[pl.ds((Q * s + j) * RB + 1, RB)]
     for cp in cpA:
         cp.wait_recv()
 
@@ -147,7 +165,8 @@
     lax.fori_loop(0, S, x_coefficients, 0)
 
     backs = []
-    for (c, jj), copies in zip(pieces, there):
+
+    def couple_piece(c, jj, copies):
         j = lax.rem(t + jj, Q)
         for cp in copies:
             cp.wait_recv()
@@ -168,10 +187,6 @@
                       for k in range(1, S)])
         xc[home] = xout[s, pl.ds(base, W)]
 
-    cpL.wait_recv()
-    cpL.wait_send()
-    sent[:] = [copy for copy in sent if copy is not cpL]
-    last[...] = jnp.where(t == 0, start_ref[...], arrived[...])
     first = lax.broadcasted_iota(jnp.int32, (N, NZ), 0) == 0
 
     def residual_row(r):
@@ -184,7 +199,8 @@
         return co(0) * ((fc_ref[r] + previous - it) - (co(1) * mk - cpl))
 
     tms = {c: [] for c in chunks}
-    for (c, jj), copies in zip(pieces, backs):
+
+    def residual_piece(c, jj, copies):
         for cp in copies:
             cp.wait_recv()
         for m in list(range(1, S)) + [0]:
@@ -198,6 +214,19 @@
                 tms[c].append(remote(res_ref.at[pl.ds(at, W)], here, {"tm": to}))
             else:
                 here[...] = res_ref[pl.ds(at, W)]
+
+    for i in range(len(pieces) + lag):
+        if i < len(pieces):
+            couple_piece(*pieces[i], there[i])
+        if i + ahead < len(pieces):
+            send_piece(*pieces[i + ahead])
+        if i == lag - 1:
+            cpL.wait_recv()
+            last[...] = jnp.where(t == 0, start_ref[...], arrived[...])
+            for copy in loads[1]:
+                copy.wait()
+        if i >= lag:
+            residual_piece(*pieces[i - lag], backs[i - lag])
 
     for cp in cpB:
         cp.wait_recv()
@@ -238,7 +267,9 @@
 
     def transform(matrix_ref, a, b, c):
         wide = jnp.concatenate([a[c * W + i] for i in range(W)], axis=1)
-        wide = jnp.dot(matrix_ref[...], wide, precision=lax.Precision.HIGHEST, preferred_element_type=jnp.float32)
+        high = wide.astype(jnp.bfloat16)
+        low = (wide - high.astype(jnp.float32)).astype(jnp.bfloat16)
+        wide = jnp.dot(matrix_ref[...], jnp.concatenate([high, low, high], axis=0), preferred_element_type=jnp.float32)
         for i in range(W):
             b[c * W + i] = wide[:, i * NZ:(i + 1) * NZ]
 
@@ -336,19 +367,19 @@
     R = RB + 2 * W
     fwd, back, shifts = step_tables(L, S)
     shifts = np.ascontiguousarray(np.broadcast_to(shifts, (3, L // 2, NZ)))
-    it = jnp.swapaxes(iterate[:, 0], 0, 1)
-    fc = jnp.swapaxes(forcing[:, 0], 0, 1)
     C = RB // W
     copies = 2 * (S - 1) + 1 + 2 * C * Q * (S - 1) + 2 * C * (S - 1) + 2 + 2 * C * (T - 1)
     f32 = jnp.float32
     vmem = lambda *shape: pltpu.VMEM(shape, f32)
     VM, SM = pl.BlockSpec(memory_space=pltpu.VMEM), pl.BlockSpec(memory_space=pltpu.SMEM)
+    ANY = pl.BlockSpec(memory_space=pl.ANY)
     res, cor = pl.pallas_call(
         functools.partial(kernel, T, S),
         out_shape=[jax.ShapeDtypeStruct((NY, N, NZ), f32)] * 2,
-        in_specs=[VM, VM, VM, VM, VM, SM, SM, VM, VM, VM],
+        in_specs=[ANY, ANY, VM, VM, VM, SM, SM, VM, VM, VM],
         out_specs=[VM, VM],
         scratch_shapes=[
+            vmem(NY, N, NZ), vmem(NY, N, NZ), pltpu.SemaphoreType.DMA((2 * N,)),
             pltpu.VMEM((2, NY + 2 * PAD, NZ), jnp.int32), vmem(NY + 2, N, NZ), vmem(NY, NZ), vmem(NY, NZ),
             pltpu.VMEM((S, 2, XB, NZ), jnp.int32), pltpu.VMEM((S, 2, RB + 2 * PAD, NZ), jnp.int32),
             vmem(S, XB, NZ), vmem(S, XB, NZ), vmem(S, XB, N, NZ), vmem(S, XB, N, NZ), vmem(NY, N, NZ),
@@ -359,7 +390,7 @@
         ],
         compiler_params=pltpu.CompilerParams(collective_id=0, has_side_effects=True, vmem_limit_bytes=48 * 2**20),
         name="all_at_once",
-    )(it, fc, start_field[0], classes[0], open_mask[0], diffusivity, drift, fwd, back, shifts)
+    )(iterate[:, 0], forcing[:, 0], start_field[0], classes[0], open_mask[0], diffusivity, drift, fwd, back, shifts)
     return jnp.swapaxes(res, 0, 1)[:, None], jnp.swapaxes(cor, 0, 1)[:, None]
 
 

time: 63.3 us -> 67.5 us (1.066)
  local copies, waits for them, and re-layouts: 4.31 us -> 9.36 us
  Pallas kernels: 58.1 us -> 56.9 us
    unnamed x18 -> x22, local copies, waits for them, and re-layouts: 2.42 us -> 9.36 us
    transpose x1 -> x0, local copies, waits for them, and re-layouts: 1.89 us -> none  [local(): fc = jnp.swapaxes(forcing[:, 0], 0, 1)]
    pallas_call x1, Pallas kernels: 58.1 us -> 56.9 us  [local(): pl.pallas_call(functools.partial(kernel, T, S), out_shape=[jax.ShapeDtype...]
where the time goes in v3:
time: 67.5 us; the launch traced here: 66.9 us
  Pallas kernels  56.9 us (84%)
  local copies, waits for them, and re-layouts  9.36 us (14%)
    pallas_call x1, Pallas kernels, local(): pl.pallas_call(functools.partial(kernel, T, S), out_shape=[jax.ShapeDtype...  56.9 us
    unnamed x22, local copies, waits for them, and re-layouts  9.36 us

profile of v3, /device:TPU:0, one launch (start us, length us, event | category | flops | bytes accessed | tf_op | source)
XLA Modules:
  0.0 66.9 jit_solution(929833622127754294)
XLA Ops:
  0.6 0.0 copy-start.8
  0.6 0.0 copy-start.9
  0.7 0.7 copy-done.8
  1.3 0.0 copy-done.9
  1.3 0.0 copy-start
  1.3 1.0 %copy-done = f32[8,1,128,128]{3,2,1,0:T(8,128)S(1)} copy-done((f32[8,1,128,128]{3,2,1,0:T(8,128)S(1)}, f32[8,1,128,128]{3,2,1,0:T(8,128)}, u32[]{:S(2)}) %copy-start) | copy-done | bytes 524312
  2.4 0.0 copy-start.1
  2.4 1.0 %copy-done.1 = f32[8,1,128,128]{3,2,1,0:T(8,128)S(1)} copy-done((f32[8,1,128,128]{3,2,1,0:T(8,128)S(1)}, f32[8,1,128,128]{3,2,1,0:T(8,128)}, u32[]{:S(2)}) %copy-start.1) | copy-done | bytes 524312
  3.4 0.0 copy-start.2
  3.4 0.8 %copy-done.2 = f32[1,128,128]{2,1,0:T(8,128)S(1)} copy-done((f32[1,128,128]{2,1,0:T(8,128)S(1)}, f32[1,128,128]{2,1,0:T(8,128)}, u32[]{:S(2)}) %copy-start.2) | copy-done | bytes 65560
  4.2 0.0 copy-start.3
  4.2 0.8 %copy-done.3 = s32[1,128,128]{2,1,0:T(8,128)S(1)} copy-done((s32[1,128,128]{2,1,0:T(8,128)S(1)}, s32[1,128,128]{2,1,0:T(8,128)}, u32[]{:S(2)}) %copy-start.3) | copy-done | bytes 65560
  5.1 0.0 copy-start.4
  5.1 0.8 %copy-done.4 = s32[1,128,128]{2,1,0:T(8,128)S(1)} copy-done((s32[1,128,128]{2,1,0:T(8,128)S(1)}, s32[1,128,128]{2,1,0:T(8,128)}, u32[]{:S(2)}) %copy-start.4) | copy-done | bytes 65560
  5.9 0.0 copy-start.5
  5.9 0.8 %copy-done.5 = f32[3,32,128]{2,1,0:T(8,128)S(1)} copy-done((f32[3,32,128]{2,1,0:T(8,128)S(1)}, f32[3,32,128]{2,1,0:T(8,128)}, u32[]{:S(2)}) %copy-start.5) | copy-done | bytes 49176
  6.7 0.0 copy-start.6
  6.7 0.8 %copy-done.6 = bf16[64,192]{1,0:T(8,128)(2,1)S(1)} copy-done((bf16[64,192]{1,0:T(8,128)(2,1)S(1)}, bf16[64,192]{1,0:T(8,128)(2,1)}, u32[]{:S(2)}) %copy-start.6) | copy-done | bytes 24600
  7.5 0.0 copy-start.7
  7.5 0.8 %copy-done.7 = bf16[64,192]{1,0:T(8,128)(2,1)S(1)} copy-done((bf16[64,192]{1,0:T(8,128)(2,1)S(1)}, bf16[64,192]{1,0:T(8,128)(2,1)}, u32[]{:S(2)}) %copy-start.7) | copy-done | bytes 24600
  8.2 56.9 %all_at_once.1 = (f32[128,8,128]{2,1,0:T(8,128)S(1)}, f32[128,8,128]{2,1,0:T(8,128)S(1)}) custom-call(f32[8,128,128]{2,1,0:T(8,128)S(1)} %bitcast.11, f32[8,128,128]{2,1,0:T(8,128)S(1)} %bitcast.12, f32[128,128]{1,0:T(8,128)S(1)} %bitcast.15, s32[128,128]{1,0:T(8,128)S(1)} %bitcast.16, s32[128,128]{1,0:T(8,128)S(1)} %bitcast.17, f32[8]{0:T(128)S(1)} %copy-done.9, ...), custom_call_target="tpu_custom_call" | custom-call | tf_op jit(solution)/shard_map/all_at_once/pallas_call | solution.py:376
  65.1 0.9 %copy.12 = f32[8,1,128,128]{3,2,1,0:T(8,128)} copy(f32[8,1,128,128]{3,0,2,1:T(8,128)S(1)} %bitcast.14) | data formatting | bytes 1048576
  66.0 0.9 %copy.13 = f32[8,1,128,128]{3,2,1,0:T(8,128)} copy(f32[8,1,128,128]{3,0,2,1:T(8,128)S(1)} %bitcast.13) | data formatting | bytes 1048576
Async XLA Ops:
  0.6 0.7 %copy-start.8 = (f32[3,8]{1,0:T(4,128)S(1)}, f32[3,8]{1,0:T(4,128)}, u32[]{:S(2)}) copy-start(f32[3,8]{1,0:T(4,128)} %drift_ref.1) | copy-start | bytes 292
  0.6 0.7 %copy-start.9 = (f32[8]{0:T(128)S(1)}, f32[8]{0:T(128)}, u32[]{:S(2)}) copy-start(f32[8]{0:T(128)} %diff_ref.1) | copy-start | bytes 100
  1.3 1.0 %copy-start = (f32[8,1,128,128]{3,2,1,0:T(8,128)S(1)}, f32[8,1,128,128]{3,2,1,0:T(8,128)}, u32[]{:S(2)}) copy-start(f32[8,1,128,128]{3,2,1,0:T(8,128)} %param.10) | copy-start | bytes 1572868
  2.4 1.0 %copy-start.1 = (f32[8,1,128,128]{3,2,1,0:T(8,128)S(1)}, f32[8,1,128,128]{3,2,1,0:T(8,128)}, u32[]{:S(2)}) copy-start(f32[8,1,128,128]{3,2,1,0:T(8,128)} %param.11) | copy-start | bytes 1572868
  3.4 0.8 %copy-start.2 = (f32[1,128,128]{2,1,0:T(8,128)S(1)}, f32[1,128,128]{2,1,0:T(8,128)}, u32[]{:S(2)}) copy-start(f32[1,128,128]{2,1,0:T(8,128)} %param.12) | copy-start | bytes 196612
  4.2 0.8 %copy-start.3 = (s32[1,128,128]{2,1,0:T(8,128)S(1)}, s32[1,128,128]{2,1,0:T(8,128)}, u32[]{:S(2)}) copy-start(s32[1,128,128]{2,1,0:T(8,128)} %param.13) | copy-start | bytes 196612
  5.1 0.8 %copy-start.4 = (s32[1,128,128]{2,1,0:T(8,128)S(1)}, s32[1,128,128]{2,1,0:T(8,128)}, u32[]{:S(2)}) copy-start(s32[1,128,128]{2,1,0:T(8,128)} %param.14) | copy-start | bytes 196612
  5.9 0.8 %copy-start.5 = (f32[3,32,128]{2,1,0:T(8,128)S(1)}, f32[3,32,128]{2,1,0:T(8,128)}, u32[]{:S(2)}) copy-start(f32[3,32,128]{2,1,0:T(8,128)} %constant.8.clone.shift_ref) | copy-start | bytes 147460
  6.7 0.8 %copy-start.6 = (bf16[64,192]{1,0:T(8,128)(2,1)S(1)}, bf16[64,192]{1,0:T(8,128)(2,1)}, u32[]{:S(2)}) copy-start(bf16[64,192]{1,0:T(8,128)(2,1)} %constant.7.clone.back_ref) | copy-start | bytes 73732
  7.5 0.8 %copy-start.7 = (bf16[64,192]{1,0:T(8,128)(2,1)S(1)}, bf16[64,192]{1,0:T(8,128)(2,1)}, u32[]{:S(2)}) copy-start(bf16[64,192]{1,0:T(8,128)(2,1)} %constant.6.clone.fwd_ref) | copy-start | bytes 73732

commit v4 on v3

--- a/solution.py
+++ b/solution.py
@@ -48,9 +48,9 @@
     return np.concatenate([high, high, low], axis=1)
 
 
-def kernel(T, S, it_in, fc_in, start_ref, cls_ref, open_ref, diff_ref, drift_ref, fwd_ref, back_ref, shift_ref,
+def kernel(T, S, it_ref, fc_ref, start_ref, cls_ref, open_ref, diff_ref, drift_ref, fwd_ref, back_ref, shift_ref,
            res_ref, cor_ref,
-           it_ref, fc_ref, in_sem, cm_ref, masked, last, arrived, cA, cB, xe, xw, xin, xout, xc, own_c, tin, spec, src, f0, f1,
+           cm_ref, masked, last, arrived, cA, cB, xe, xw, xin, xout, xc, own_c, tin, spec, src, f0, f1,
            sol_c, inv, spec2, outb, ssem, rsem):
     NY, N, NZ = it_ref.shape
     L = N * T
@@ -61,14 +61,8 @@
     W = SWEEPS
     R = RB + 2 * W
     C = RB // W
-    chunks = [0, C - 1] + list(range(1, C - 1))
+    chunks = [0, C - 1][:C] + list(range(1, C - 1))
     t, s = lax.axis_index("tm"), lax.axis_index("space")
-
-    loads = []
-    for i, (a, b) in enumerate(((it_in, it_ref), (fc_in, fc_ref))):
-        loads.append([pltpu.make_async_copy(a.at[n], b.at[:, n, :], in_sem.at[i * N + n]) for n in range(N)])
-        for copy in loads[i]:
-            copy.start()
 
     barrier = pltpu.get_barrier_semaphore()
     for k in range(1, S):
@@ -120,15 +114,13 @@
     masked[0] = zero
     masked[NY + 1] = zero
 
-    for copy in loads[0]:
-        copy.wait()
-
     def mask_row(r, c):
         masked[r + 1] = it_ref[r] * own_c[0, pl.ds(r, 1), :]
         return c
 
     lax.fori_loop(0, NY, mask_row, 0, unroll=8)
 
+    last[...] = it_ref[:, N - 1, :]
     pl.semaphore_wait(barrier, S - 1 + T - 1)
 
     cpA = [remote(cm_ref.at[:, pl.ds(mult(lax.rem(s + k, S) * XB + PAD, 8), XB)], cA.at[s],
@@ -145,7 +137,7 @@
     ahead, lag = 4, 2
     for piece in pieces[:ahead]:
         send_piece(*piece)
-    cpL = remote(it_in.at[N - 1], arrived, {"tm": lax.rem(t + 1, T)})
+    cpL = remote(last, arrived, {"tm": lax.rem(t + 1, T)})
     cpB = [remote(cm_ref.at[:, pl.ds(mult(RB * t, 8), RB + 2 * PAD)], cB.at[s], {"space": lax.rem(s + k, S)})
            for k in range(1, S)]
 
@@ -193,7 +185,7 @@
         it = it_ref[r]
         mk = masked[r + 1]
         co = lambda i: own_c[i, pl.ds(r, 1), :]
-        previous = jnp.where(first, last[pl.ds(r, 1), :], pltpu.roll(it, 1, 0))
+        previous = jnp.where(first, arrived[pl.ds(r, 1), :], pltpu.roll(it, 1, 0))
         cpl = co(2) * masked[r + 2] + co(3) * masked[r] + xc[r]
         cpl = cpl + co(4) * pltpu.roll(mk, NZ - 1, 1) + co(5) * pltpu.roll(mk, 1, 1)
         return co(0) * ((fc_ref[r] + previous - it) - (co(1) * mk - cpl))
@@ -222,9 +214,7 @@
             send_piece(*pieces[i + ahead])
         if i == lag - 1:
             cpL.wait_recv()
-            last[...] = jnp.where(t == 0, start_ref[...], arrived[...])
-            for copy in loads[1]:
-                copy.wait()
+            arrived[...] = jnp.where(t == 0, start_ref[...], arrived[...])
         if i >= lag:
             residual_piece(*pieces[i - lag], backs[i - lag])
 
@@ -366,20 +356,20 @@
     H, W = G // 2, SWEEPS
     R = RB + 2 * W
     fwd, back, shifts = step_tables(L, S)
+    it = jnp.swapaxes(iterate[:, 0], 0, 1)
+    fc = jnp.swapaxes(forcing[:, 0], 0, 1)
     shifts = np.ascontiguousarray(np.broadcast_to(shifts, (3, L // 2, NZ)))
     C = RB // W
     copies = 2 * (S - 1) + 1 + 2 * C * Q * (S - 1) + 2 * C * (S - 1) + 2 + 2 * C * (T - 1)
     f32 = jnp.float32
     vmem = lambda *shape: pltpu.VMEM(shape, f32)
     VM, SM = pl.BlockSpec(memory_space=pltpu.VMEM), pl.BlockSpec(memory_space=pltpu.SMEM)
-    ANY = pl.BlockSpec(memory_space=pl.ANY)
     res, cor = pl.pallas_call(
         functools.partial(kernel, T, S),
         out_shape=[jax.ShapeDtypeStruct((NY, N, NZ), f32)] * 2,
-        in_specs=[ANY, ANY, VM, VM, VM, SM, SM, VM, VM, VM],
+        in_specs=[VM, VM, VM, VM, VM, SM, SM, VM, VM, VM],
         out_specs=[VM, VM],
         scratch_shapes=[
-            vmem(NY, N, NZ), vmem(NY, N, NZ), pltpu.SemaphoreType.DMA((2 * N,)),
             pltpu.VMEM((2, NY + 2 * PAD, NZ), jnp.int32), vmem(NY + 2, N, NZ), vmem(NY, NZ), vmem(NY, NZ),
             pltpu.VMEM((S, 2, XB, NZ), jnp.int32), pltpu.VMEM((S, 2, RB + 2 * PAD, NZ), jnp.int32),
             vmem(S, XB, NZ), vmem(S, XB, NZ), vmem(S, XB, N, NZ), vmem(S, XB, N, NZ), vmem(NY, N, NZ),
@@ -390,7 +380,7 @@
         ],
         compiler_params=pltpu.CompilerParams(collective_id=0, has_side_effects=True, vmem_limit_bytes=48 * 2**20),
         name="all_at_once",
-    )(iterate[:, 0], forcing[:, 0], start_field[0], classes[0], open_mask[0], diffusivity, drift, fwd, back, shifts)
+    )(it, fc, start_field[0], classes[0], open_mask[0], diffusivity, drift, fwd, back, shifts)
     return jnp.swapaxes(res, 0, 1)[:, None], jnp.swapaxes(cor, 0, 1)[:, None]
 
 

time: 67.5 us -> 61.2 us (0.907)
  local copies, waits for them, and re-layouts: 9.36 us -> 4.31 us
  Pallas kernels: 56.9 us -> 56 us
    unnamed x22 -> x18, local copies, waits for them, and re-layouts: 9.36 us -> 2.42 us
    transpose x0 -> x1, local copies, waits for them, and re-layouts: none -> 1.89 us  [local(): fc = jnp.swapaxes(forcing[:, 0], 0, 1)]
    pallas_call x1, Pallas kernels: 56.9 us -> 56 us  [local(): pl.pallas_call(functools.partial(kernel, T, S), out_shape=[jax.ShapeDtype...]
where the time goes in v4:
time: 61.2 us; the launch traced here: 61.1 us
  Pallas kernels  56 us (92%)
  local copies, waits for them, and re-layouts  4.31 us (7%)
  between operations  0.75 us (1%)
    pallas_call x1, Pallas kernels, local(): pl.pallas_call(functools.partial(kernel, T, S), out_shape=[jax.ShapeDtype...  56 us
    unnamed x18, local copies, waits for them, and re-layouts  2.42 us
    transpose x1, local copies, waits for them, and re-layouts, local(): fc = jnp.swapaxes(forcing[:, 0], 0, 1)  1.89 us

profile of v4, /device:TPU:0, one launch (start us, length us, event | category | flops | bytes accessed | tf_op | source)
XLA Modules:
  0.0 61.1 jit_solution(1913186747480369742)
XLA Ops:
  0.6 0.0 copy-start
  0.6 0.0 copy-start.1
  0.7 0.0 copy-start.2
  0.7 0.0 copy-start.3
  0.7 0.0 copy-start.4
  0.7 0.0 copy-start.5
  0.7 1.9 %copy_bitcast_fusion = (f32[128,8,128]{2,1,0:T(8,128)S(1)}, f32[128,8,128]{2,1,0:T(8,128)S(1)}) fusion(f32[8,1,128,128]{3,2,1,0:T(8,128)} %param.11, f32[8,1,128,128]{3,2,1,0:T(8,128)} %param.10), kind=kLoop, calls=%fused_computation | loop fusion | bytes 2097152 | tf_op jit(solution)/shard_map/transpose | solution.py:360
  2.6 0.0 copy-start.6
  2.6 0.0 copy-start.7
  2.6 0.0 copy-done
  2.6 0.0 copy-done.1
  2.6 0.0 copy-done.2
  2.6 0.0 copy-done.3
  2.7 0.0 copy-done.4
  2.7 0.0 copy-done.5
  2.7 0.6 copy-done.6
  3.3 0.0 copy-done.7
  3.3 56.0 %all_at_once.1 = (f32[128,8,128]{2,1,0:T(8,128)S(1)}, f32[128,8,128]{2,1,0:T(8,128)S(1)}) custom-call(f32[128,8,128]{2,1,0:T(8,128)S(1)} %get-tuple-element.9.it_ref, f32[128,8,128]{2,1,0:T(8,128)S(1)} %get-tuple-element.8.fc_ref, f32[128,128]{1,0:T(8,128)S(1)} %bitcast.19, s32[128,128]{1,0:T(8,128)S(1)} %bitcast.20, s32[128,128]{1,0:T(8,128)S(1)} %bitcast.21, ...), custom_call_target="tpu_custom_call" | custom-call | tf_op jit(solution)/shard_map/all_at_once/pallas_call | solution.py:367
  59.3 0.9 %copy.14 = f32[8,1,128,128]{3,2,1,0:T(8,128)} copy(f32[8,1,128,128]{3,0,2,1:T(8,128)S(1)} %bitcast.18) | data formatting | bytes 1048576
  60.2 0.9 %copy.15 = f32[8,1,128,128]{3,2,1,0:T(8,128)} copy(f32[8,1,128,128]{3,0,2,1:T(8,128)S(1)} %bitcast.17) | data formatting | bytes 1048576
Async XLA Ops:
  0.6 2.0 %copy-start = (f32[1,128,128]{2,1,0:T(8,128)S(1)}, f32[1,128,128]{2,1,0:T(8,128)}, u32[]{:S(2)}) copy-start(f32[1,128,128]{2,1,0:T(8,128)} %param.12) | copy-start | bytes 196612
  0.6 2.0 %copy-start.1 = (s32[1,128,128]{2,1,0:T(8,128)S(1)}, s32[1,128,128]{2,1,0:T(8,128)}, u32[]{:S(2)}) copy-start(s32[1,128,128]{2,1,0:T(8,128)} %param.13) | copy-start | bytes 196612
  0.7 2.0 %copy-start.2 = (s32[1,128,128]{2,1,0:T(8,128)S(1)}, s32[1,128,128]{2,1,0:T(8,128)}, u32[]{:S(2)}) copy-start(s32[1,128,128]{2,1,0:T(8,128)} %param.14) | copy-start | bytes 196612
  0.7 2.0 %copy-start.3 = (f32[3,32,128]{2,1,0:T(8,128)S(1)}, f32[3,32,128]{2,1,0:T(8,128)}, u32[]{:S(2)}) copy-start(f32[3,32,128]{2,1,0:T(8,128)} %constant.8.clone.shift_ref) | copy-start | bytes 147460
  0.7 2.0 %copy-start.4 = (bf16[64,192]{1,0:T(8,128)(2,1)S(1)}, bf16[64,192]{1,0:T(8,128)(2,1)}, u32[]{:S(2)}) copy-start(bf16[64,192]{1,0:T(8,128)(2,1)} %constant.7.clone.back_ref) | copy-start | bytes 73732
  0.7 2.0 %copy-start.5 = (bf16[64,192]{1,0:T(8,128)(2,1)S(1)}, bf16[64,192]{1,0:T(8,128)(2,1)}, u32[]{:S(2)}) copy-start(bf16[64,192]{1,0:T(8,128)(2,1)} %constant.6.clone.fwd_ref) | copy-start | bytes 73732
  2.6 0.7 %copy-start.6 = (f32[3,8]{1,0:T(4,128)S(1)}, f32[3,8]{1,0:T(4,128)}, u32[]{:S(2)}) copy-start(f32[3,8]{1,0:T(4,128)} %drift_ref.1) | copy-start | bytes 292
  2.6 0.7 %copy-start.7 = (f32[8]{0:T(128)S(1)}, f32[8]{0:T(128)}, u32[]{:S(2)}) copy-start(f32[8]{0:T(128)} %diff_ref.1) | copy-start | bytes 100

commit v5 on v4

--- a/solution.py
+++ b/solution.py
@@ -134,7 +134,7 @@
                              xin.at[s, pl.ds(jj * RB + c * W, W)], {"space": lax.rem(s + k, S)}) for k in range(1, S)])
         xin[s, pl.ds(jj * RB + c * W, W)] = masked[pl.ds((Q * s + j) * RB + c * W + 1, W)]
 
-    ahead, lag = 4, 2
+    ahead, lag = 4, 1
     for piece in pieces[:ahead]:
         send_piece(*piece)
     cpL = remote(last, arrived, {"tm": lax.rem(t + 1, T)})
@@ -285,7 +285,7 @@
             halos.append(remote(src.at[:, pl.ds(W, W)], src.at[:, pl.ds(RB + W, W)], {"tm": lax.rem(t + T - 1, T)}))
         if c == C - 1:
             halos.append(remote(src.at[:, pl.ds(RB, W)], src.at[:, pl.ds(0, W)], {"tm": lax.rem(t + 1, T)}))
-        lax.fori_loop(W + c * W, W + c * W + W, first_row, 0, unroll=2)
+        lax.fori_loop(W + c * W, W + c * W + W, first_row, 0, unroll=4)
 
     flying = []
     for c in chunks:
@@ -325,7 +325,7 @@
             lax.fori_loop(sweep, R - sweep, sweep_row, 0, unroll=2)
         else:
             for c in range(C):
-                lax.fori_loop(W + c * W, W + c * W + W, sweep_row, 0, unroll=2)
+                lax.fori_loop(W + c * W, W + c * W + W, sweep_row, 0, unroll=4)
                 rows, from_rows = pl.ds(c * W, W), pl.ds(W + c * W, W)
                 solved.append([remote(new.at[lax.rem(s + k, S), from_rows], spec2.at[rows, planes(s), :],
                                       {"space": lax.rem(s + k, S)}) for k in range(1, S)])

time: 61.2 us -> 64.5 us (1.054)
  Pallas kernels: 56 us -> 59.3 us
    pallas_call x1, Pallas kernels: 56 us -> 59.3 us  [local(): pl.pallas_call(functools.partial(kernel, T, S), out_shape=[jax.ShapeDtype...]
where the time goes in v5:
time: 64.5 us; the launch traced here: 64.4 us
  Pallas kernels  59.3 us (92%)
  local copies, waits for them, and re-layouts  4.31 us (7%)
  between operations  0.75 us (1%)
    pallas_call x1, Pallas kernels, local(): pl.pallas_call(functools.partial(kernel, T, S), out_shape=[jax.ShapeDtype...  59.3 us
    unnamed x18, local copies, waits for them, and re-layouts  2.42 us
    transpose x1, local copies, waits for them, and re-layouts, local(): fc = jnp.swapaxes(forcing[:, 0], 0, 1)  1.89 us

profile of v5, /device:TPU:0, one launch (start us, length us, event | category | flops | bytes accessed | tf_op | source)
XLA Modules:
  0.0 64.4 jit_solution(15399396809672971026)
XLA Ops:
  0.6 0.0 copy-start
  0.6 0.0 copy-start.1
  0.7 0.0 copy-start.2
  0.7 0.0 copy-start.3
  0.7 0.0 copy-start.4
  0.7 0.0 copy-start.5
  0.7 1.9 %copy_bitcast_fusion = (f32[128,8,128]{2,1,0:T(8,128)S(1)}, f32[128,8,128]{2,1,0:T(8,128)S(1)}) fusion(f32[8,1,128,128]{3,2,1,0:T(8,128)} %param.11, f32[8,1,128,128]{3,2,1,0:T(8,128)} %param.10), kind=kLoop, calls=%fused_computation | loop fusion | bytes 2097152 | tf_op jit(solution)/shard_map/transpose | solution.py:360
  2.6 0.0 copy-start.6
  2.6 0.0 copy-start.7
  2.6 0.0 copy-done
  2.6 0.0 copy-done.1
  2.6 0.0 copy-done.2
  2.6 0.0 copy-done.3
  2.7 0.0 copy-done.4
  2.7 0.0 copy-done.5
  2.7 0.6 copy-done.6
  3.3 0.0 copy-done.7
  3.3 59.3 %all_at_once.1 = (f32[128,8,128]{2,1,0:T(8,128)S(1)}, f32[128,8,128]{2,1,0:T(8,128)S(1)}) custom-call(f32[128,8,128]{2,1,0:T(8,128)S(1)} %get-tuple-element.9.it_ref, f32[128,8,128]{2,1,0:T(8,128)S(1)} %get-tuple-element.8.fc_ref, f32[128,128]{1,0:T(8,128)S(1)} %bitcast.19, s32[128,128]{1,0:T(8,128)S(1)} %bitcast.20, s32[128,128]{1,0:T(8,128)S(1)} %bitcast.21, ...), custom_call_target="tpu_custom_call" | custom-call | tf_op jit(solution)/shard_map/all_at_once/pallas_call | solution.py:367
  62.6 0.9 %copy.14 = f32[8,1,128,128]{3,2,1,0:T(8,128)} copy(f32[8,1,128,128]{3,0,2,1:T(8,128)S(1)} %bitcast.18) | data formatting | bytes 1048576
  63.5 0.9 %copy.15 = f32[8,1,128,128]{3,2,1,0:T(8,128)} copy(f32[8,1,128,128]{3,0,2,1:T(8,128)S(1)} %bitcast.17) | data formatting | bytes 1048576
Async XLA Ops:
  0.6 2.0 %copy-start = (f32[1,128,128]{2,1,0:T(8,128)S(1)}, f32[1,128,128]{2,1,0:T(8,128)}, u32[]{:S(2)}) copy-start(f32[1,128,128]{2,1,0:T(8,128)} %param.12) | copy-start | bytes 196612
  0.6 2.0 %copy-start.1 = (s32[1,128,128]{2,1,0:T(8,128)S(1)}, s32[1,128,128]{2,1,0:T(8,128)}, u32[]{:S(2)}) copy-start(s32[1,128,128]{2,1,0:T(8,128)} %param.13) | copy-start | bytes 196612
  0.7 2.0 %copy-start.2 = (s32[1,128,128]{2,1,0:T(8,128)S(1)}, s32[1,128,128]{2,1,0:T(8,128)}, u32[]{:S(2)}) copy-start(s32[1,128,128]{2,1,0:T(8,128)} %param.14) | copy-start | bytes 196612
  0.7 2.0 %copy-start.3 = (f32[3,32,128]{2,1,0:T(8,128)S(1)}, f32[3,32,128]{2,1,0:T(8,128)}, u32[]{:S(2)}) copy-start(f32[3,32,128]{2,1,0:T(8,128)} %constant.8.clone.shift_ref) | copy-start | bytes 147460
  0.7 2.0 %copy-start.4 = (bf16[64,192]{1,0:T(8,128)(2,1)S(1)}, bf16[64,192]{1,0:T(8,128)(2,1)}, u32[]{:S(2)}) copy-start(bf16[64,192]{1,0:T(8,128)(2,1)} %constant.7.clone.back_ref) | copy-start | bytes 73732
  0.7 2.0 %copy-start.5 = (bf16[64,192]{1,0:T(8,128)(2,1)S(1)}, bf16[64,192]{1,0:T(8,128)(2,1)}, u32[]{:S(2)}) copy-start(bf16[64,192]{1,0:T(8,128)(2,1)} %constant.6.clone.fwd_ref) | copy-start | bytes 73732
  2.6 0.7 %copy-start.6 = (f32[3,8]{1,0:T(4,128)S(1)}, f32[3,8]{1,0:T(4,128)}, u32[]{:S(2)}) copy-start(f32[3,8]{1,0:T(4,128)} %drift_ref.1) | copy-start | bytes 292
  2.6 0.7 %copy-start.7 = (f32[8]{0:T(128)S(1)}, f32[8]{0:T(128)}, u32[]{:S(2)}) copy-start(f32[8]{0:T(128)} %diff_ref.1) | copy-start | bytes 100
